TPU v7x, 512 devices: a whole 4x8x8 slice. The times are simulated.
512 devices in a mesh: grp: 16 (over y, x_lo), blk: 32 (over z, x_hi, core).
Axes of the slice: x: 4 (x_hi: 2, x_lo: 2; x = x_hi * 2 + x_lo), y: 8, z: 8, core: 2. Of those that a mesh axis runs over, the one named last changes fastest.
Arguments:
- tile_values: bfloat16 [512, 6, 256, 256], P(('grp', 'blk')), may hold values from 0.019897461 to 1
- tile_offset: int32 [512, 6], P(('grp', 'blk')), may hold values from 0 to 7, as said below
- tile_exponent: int32 [512, 6], P(('grp', 'blk')), may hold values from -2 to 2
- initial_vectors: bfloat16 [131072, 64], P(('grp', 'blk')), may hold values from -6 to 6
Outputs:
- spectral_vectors: float32 [131072, 64], P(('grp', 'blk'))
Inputs may be any that keep to these rules, and one draw needn't show every extreme that they name: `tile_offset`: in each row slot 0 holds 0 and the offsets are distinct and ascending.
All inputs are finite; a program needn't handle non-finite values.
Results may differ from a plain program's by a relative error of at most 0.0041.
Values may be sent and summed in bfloat16 or wider, within the bound.
A program may use at most 64 MiB of HBM per device.

v0:
```python
import jax
import jax.numpy as jnp
from jax import lax
from jax.sharding import PartitionSpec as P


def from_behind(block, axis, distance):
    devices = range(lax.axis_size(axis))
    route = [((i - distance) % len(devices), i) for i in devices]
    return lax.ppermute(block, axis, route)


def power_of_two(exponent):
    return jnp.where(
        exponent == -2,
        0.25,
        jnp.where(
            exponent == -1, 0.5, jnp.where(exponent == 0, 1.0, jnp.where(exponent == 1, 2.0, 4.0))
        ),
    ).astype(jnp.float32)


def orthonormal(image):
    local_gram = jnp.dot(
        image.T, image, precision=lax.Precision.HIGHEST, preferred_element_type=jnp.float32
    )
    total_nodes = image.shape[0] * lax.axis_size("grp") * lax.axis_size("blk")
    gram_matrix = lax.psum(local_gram, ("grp", "blk")) / total_nodes
    factor_lower = jnp.linalg.cholesky(gram_matrix)
    return jax.scipy.linalg.solve_triangular(factor_lower, image.T, lower=True).T


def absorb(paths, values, offsets, step, scaled, own_offset):
    selector = (own_offset == step).astype(jnp.bfloat16)
    left = jnp.einsum("b,bij->ij", selector, scaled, preferred_element_type=jnp.float32).astype(
        jnp.bfloat16
    )
    meets = step + offsets[None, :] == own_offset[:, None]
    right = jnp.einsum(
        "ac,cij->aij", meets.astype(jnp.bfloat16), values, preferred_element_type=jnp.float32
    ).astype(jnp.bfloat16)
    return paths + jnp.einsum("ij,ajk->aik", left, right, preferred_element_type=jnp.float32)


def shards(tile_values, tile_offset, tile_exponent, initial_vectors):
    cycle_size = lax.axis_size("blk")
    reach = min(8, cycle_size // 2)
    own_offset = tile_offset[0]
    scale = power_of_two(tile_exponent[0])
    scaled = (tile_values[0].astype(jnp.float32) * scale[:, None, None]).astype(jnp.bfloat16)
    marks = own_offset.astype(jnp.bfloat16)
    paths = absorb(jnp.zeros(scaled.shape, jnp.float32), scaled, own_offset, 0, scaled, own_offset)

    def cycle_step(step, carry):
        running, moving_values, moving_marks = carry
        moving_values, moving_marks = from_behind((moving_values, moving_marks), "blk", -1)
        running = absorb(
            running, moving_values, moving_marks.astype(jnp.int32), step, scaled, own_offset
        )
        return (running, moving_values, moving_marks)

    paths = lax.fori_loop(1, reach, cycle_step, (paths, scaled, marks))[0]
    motif = (scaled.astype(jnp.float32) * paths).astype(jnp.bfloat16)
    degree = jnp.sum(motif, axis=(0, 2), dtype=jnp.float32)

    def picked_tile(step):
        selector = (own_offset == step).astype(jnp.bfloat16)
        return jnp.einsum("a,aij->ij", selector, motif, preferred_element_type=jnp.float32).astype(
            jnp.bfloat16
        )

    basis = initial_vectors.astype(jnp.float32)
    for turn in range(2):
        current = (basis * lax.rsqrt(degree)[:, None]).astype(jnp.bfloat16)

        def vector_step(step, carry):
            running, piece = carry
            piece = from_behind(piece, "blk", -1)
            running = running + jnp.dot(
                picked_tile(step), piece, preferred_element_type=jnp.float32
            )
            return (running, piece)

        first = jnp.dot(picked_tile(0), current, preferred_element_type=jnp.float32)
        total = lax.fori_loop(1, reach, vector_step, (first, current))[0]
        image = total + degree[:, None] * current.astype(jnp.float32)
        basis = orthonormal(image * lax.rsqrt(degree)[:, None])
    return basis


def solution(mesh):
    return jax.shard_map(
        shards,
        mesh=mesh,
        in_specs=(
            P(("grp", "blk"), None, None, None),
            P(("grp", "blk"), None),
            P(("grp", "blk"), None),
            P(("grp", "blk"), None),
        ),
        out_specs=P(("grp", "blk"), None),
        check_vma=False,
    )
```

profile of v0, /device:TPU:1, one launch (start us, length us, event | category | flops | bytes accessed | tf_op | source)
XLA Modules:
  0.0 517.8 jit_solution(17186598564516200930)
XLA Ops:
  6.1 150.9 %while.47 = (s32[]{:T(128)}, f32[6,256,256]{1,2,0:T(8,128)}, bf16[6,256,256]{2,1,0:T(8,128)(2,1)S(1)}, bf16[6]{0:T(256)(128)(2,1)S(1)}, s32[1,6]{1,0:T(1,128)S(1...) while((s32[]{:T(128)}, f32[6,256,256]{1,2,0:T(8,128)}, ...), condition=%wide.region_1.2_spmd, body=%wide.region_0.1_spmd.sunk | while | flops 207224880 | bytes 12845409 | solution.py:62
  6.1 8.8 %collective-permute-start = (bf16[6,256,256]{2,1,0:T(8,128)(2,1)S(1)}, bf16[6,256,256]{2,1,0:T(8,128)(2,1)S(1)}, u32[]{:S(2)}, u32[]{:S(2)}) collective-permute-start(bf16[6,256,256]{2,1,0:T(8,128)(2,1)S(1)} %get-tuple-element.483), channel_id=1, source_target_pairs={{1,0},{2,1},{3,2},{4,3},{5,4},{6,5},{7,6},{8,7},{9,8},{10,9},{11,1... | collective-permute-start | bytes 2359304 | tf_op jit(solution)/shard_map/while/body/eval_jaxpr/ppermute | solution.py:10
  14.9 7.5 %collective-permute-start.1 = (bf16[6]{0:T(256)(128)(2,1)S(1)}, bf16[6]{0:T(256)(128)(2,1)S(1)}, u32[]{:S(2)}, u32[]{:S(2)}) collective-permute-start(bf16[6]{0:T(256)(128)(2,1)S(1)} %get-tuple-element.484), channel_id=1, source_target_pairs={{1,0},{2,1},{3,2},{4,3},{5,4},{6,5},{7,6},{8,7},{9,8},{10,9},{11,1... | collective-permute-start | bytes 44 | tf_op jit(solution)/shard_map/while/body/eval_jaxpr/ppermute | solution.py:10
  28.2 8.2 %collective-permute-start = (bf16[6,256,256]{2,1,0:T(8,128)(2,1)S(1)}, bf16[6,256,256]{2,1,0:T(8,128)(2,1)S(1)}, u32[]{:S(2)}, u32[]{:S(2)}) collective-permute-start(bf16[6,256,256]{2,1,0:T(8,128)(2,1)S(1)} %get-tuple-element.483), channel_id=1, source_target_pairs={{1,0},{2,1},{3,2},{4,3},{5,4},{6,5},{7,6},{8,7},{9,8},{10,9},{11,1... | collective-permute-start | bytes 2359304 | tf_op jit(solution)/shard_map/while/body/eval_jaxpr/ppermute | solution.py:10
  49.7 8.2 %collective-permute-start = (bf16[6,256,256]{2,1,0:T(8,128)(2,1)S(1)}, bf16[6,256,256]{2,1,0:T(8,128)(2,1)S(1)}, u32[]{:S(2)}, u32[]{:S(2)}) collective-permute-start(bf16[6,256,256]{2,1,0:T(8,128)(2,1)S(1)} %get-tuple-element.483), channel_id=1, source_target_pairs={{1,0},{2,1},{3,2},{4,3},{5,4},{6,5},{7,6},{8,7},{9,8},{10,9},{11,1... | collective-permute-start | bytes 2359304 | tf_op jit(solution)/shard_map/while/body/eval_jaxpr/ppermute | solution.py:10
  71.2 8.2 %collective-permute-start = (bf16[6,256,256]{2,1,0:T(8,128)(2,1)S(1)}, bf16[6,256,256]{2,1,0:T(8,128)(2,1)S(1)}, u32[]{:S(2)}, u32[]{:S(2)}) collective-permute-start(bf16[6,256,256]{2,1,0:T(8,128)(2,1)S(1)} %get-tuple-element.483), channel_id=1, source_target_pairs={{1,0},{2,1},{3,2},{4,3},{5,4},{6,5},{7,6},{8,7},{9,8},{10,9},{11,1... | collective-permute-start | bytes 2359304 | tf_op jit(solution)/shard_map/while/body/eval_jaxpr/ppermute | solution.py:10
  79.3 7.5 %collective-permute-start.1 = (bf16[6]{0:T(256)(128)(2,1)S(1)}, bf16[6]{0:T(256)(128)(2,1)S(1)}, u32[]{:S(2)}, u32[]{:S(2)}) collective-permute-start(bf16[6]{0:T(256)(128)(2,1)S(1)} %get-tuple-element.484), channel_id=1, source_target_pairs={{1,0},{2,1},{3,2},{4,3},{5,4},{6,5},{7,6},{8,7},{9,8},{10,9},{11,1... | collective-permute-start | bytes 44 | tf_op jit(solution)/shard_map/while/body/eval_jaxpr/ppermute | solution.py:10
  92.6 8.2 %collective-permute-start = (bf16[6,256,256]{2,1,0:T(8,128)(2,1)S(1)}, bf16[6,256,256]{2,1,0:T(8,128)(2,1)S(1)}, u32[]{:S(2)}, u32[]{:S(2)}) collective-permute-start(bf16[6,256,256]{2,1,0:T(8,128)(2,1)S(1)} %get-tuple-element.483), channel_id=1, source_target_pairs={{1,0},{2,1},{3,2},{4,3},{5,4},{6,5},{7,6},{8,7},{9,8},{10,9},{11,1... | collective-permute-start | bytes 2359304 | tf_op jit(solution)/shard_map/while/body/eval_jaxpr/ppermute | solution.py:10
  114.1 8.2 %collective-permute-start = (bf16[6,256,256]{2,1,0:T(8,128)(2,1)S(1)}, bf16[6,256,256]{2,1,0:T(8,128)(2,1)S(1)}, u32[]{:S(2)}, u32[]{:S(2)}) collective-permute-start(bf16[6,256,256]{2,1,0:T(8,128)(2,1)S(1)} %get-tuple-element.483), channel_id=1, source_target_pairs={{1,0},{2,1},{3,2},{4,3},{5,4},{6,5},{7,6},{8,7},{9,8},{10,9},{11,1... | collective-permute-start | bytes 2359304 | tf_op jit(solution)/shard_map/while/body/eval_jaxpr/ppermute | solution.py:10
  122.3 7.5 %collective-permute-start.1 = (bf16[6]{0:T(256)(128)(2,1)S(1)}, bf16[6]{0:T(256)(128)(2,1)S(1)}, u32[]{:S(2)}, u32[]{:S(2)}) collective-permute-start(bf16[6]{0:T(256)(128)(2,1)S(1)} %get-tuple-element.484), channel_id=1, source_target_pairs={{1,0},{2,1},{3,2},{4,3},{5,4},{6,5},{7,6},{8,7},{9,8},{10,9},{11,1... | collective-permute-start | bytes 44 | tf_op jit(solution)/shard_map/while/body/eval_jaxpr/ppermute | solution.py:10
  135.6 8.2 %collective-permute-start = (bf16[6,256,256]{2,1,0:T(8,128)(2,1)S(1)}, bf16[6,256,256]{2,1,0:T(8,128)(2,1)S(1)}, u32[]{:S(2)}, u32[]{:S(2)}) collective-permute-start(bf16[6,256,256]{2,1,0:T(8,128)(2,1)S(1)} %get-tuple-element.483), channel_id=1, source_target_pairs={{1,0},{2,1},{3,2},{4,3},{5,4},{6,5},{7,6},{8,7},{9,8},{10,9},{11,1... | collective-permute-start | bytes 2359304 | tf_op jit(solution)/shard_map/while/body/eval_jaxpr/ppermute | solution.py:10
  160.7 66.0 %while.48 = (s32[]{:T(128)}, f32[256,64]{0,1:T(8,128)S(1)}, bf16[256,64]{1,0:T(8,128)(2,1)S(1)}, s32[6]{0:T(128)S(1)}, bf16[6,256,256]{2,1,0:T(8,128)(2,1)S(1)}, /*index=5*/s32[]{:T(128)}) while((s32[]{:T(128)}, f32[256,64]{0,1:T(8,128)S(1)}, bf16[256,64]{1,0:T(8,128)(2,1)S(1)}, s32[6]{0:T(128)S(1)}, bf16[6,256,256]{2,1,0:T(8,128)(2,1)S(1)}, ...), condition=%wide.region_4.5_spmd, body=%wide.region_3.4_spmd.sunk | while | flops 9191432 | bytes 1409161 | solution.py:85
  160.7 8.2 %collective-permute-start.2 = (bf16[256,64]{1,0:T(8,128)(2,1)S(1)}, bf16[256,64]{1,0:T(8,128)(2,1)S(1)}, u32[]{:S(2)}, u32[]{:S(2)}) collective-permute-start(bf16[256,64]{1,0:T(8,128)(2,1)S(1)} %get-tuple-element.505), channel_id=1, source_target_pairs={{1,0},{2,1},{3,2},{4,3},{5,4},{6,5},{7,6},{8,7},{9,8},{10,9},{11,1... | collective-permute-start | bytes 98312 | tf_op jit(solution)/shard_map/while/body/eval_jaxpr/ppermute | solution.py:10
  170.0 8.5 %collective-permute-start.2 = (bf16[256,64]{1,0:T(8,128)(2,1)S(1)}, bf16[256,64]{1,0:T(8,128)(2,1)S(1)}, u32[]{:S(2)}, u32[]{:S(2)}) collective-permute-start(bf16[256,64]{1,0:T(8,128)(2,1)S(1)} %get-tuple-element.505), channel_id=1, source_target_pairs={{1,0},{2,1},{3,2},{4,3},{5,4},{6,5},{7,6},{8,7},{9,8},{10,9},{11,1... | collective-permute-start | bytes 98312 | tf_op jit(solution)/shard_map/while/body/eval_jaxpr/ppermute | solution.py:10
  179.6 8.3 %collective-permute-start.2 = (bf16[256,64]{1,0:T(8,128)(2,1)S(1)}, bf16[256,64]{1,0:T(8,128)(2,1)S(1)}, u32[]{:S(2)}, u32[]{:S(2)}) collective-permute-start(bf16[256,64]{1,0:T(8,128)(2,1)S(1)} %get-tuple-element.505), channel_id=1, source_target_pairs={{1,0},{2,1},{3,2},{4,3},{5,4},{6,5},{7,6},{8,7},{9,8},{10,9},{11,1... | collective-permute-start | bytes 98312 | tf_op jit(solution)/shard_map/while/body/eval_jaxpr/ppermute | solution.py:10
  189.0 8.3 %collective-permute-start.2 = (bf16[256,64]{1,0:T(8,128)(2,1)S(1)}, bf16[256,64]{1,0:T(8,128)(2,1)S(1)}, u32[]{:S(2)}, u32[]{:S(2)}) collective-permute-start(bf16[256,64]{1,0:T(8,128)(2,1)S(1)} %get-tuple-element.505), channel_id=1, source_target_pairs={{1,0},{2,1},{3,2},{4,3},{5,4},{6,5},{7,6},{8,7},{9,8},{10,9},{11,1... | collective-permute-start | bytes 98312 | tf_op jit(solution)/shard_map/while/body/eval_jaxpr/ppermute | solution.py:10
  198.5 8.3 %collective-permute-start.2 = (bf16[256,64]{1,0:T(8,128)(2,1)S(1)}, bf16[256,64]{1,0:T(8,128)(2,1)S(1)}, u32[]{:S(2)}, u32[]{:S(2)}) collective-permute-start(bf16[256,64]{1,0:T(8,128)(2,1)S(1)} %get-tuple-element.505), channel_id=1, source_target_pairs={{1,0},{2,1},{3,2},{4,3},{5,4},{6,5},{7,6},{8,7},{9,8},{10,9},{11,1... | collective-permute-start | bytes 98312 | tf_op jit(solution)/shard_map/while/body/eval_jaxpr/ppermute | solution.py:10
  207.9 8.3 %collective-permute-start.2 = (bf16[256,64]{1,0:T(8,128)(2,1)S(1)}, bf16[256,64]{1,0:T(8,128)(2,1)S(1)}, u32[]{:S(2)}, u32[]{:S(2)}) collective-permute-start(bf16[256,64]{1,0:T(8,128)(2,1)S(1)} %get-tuple-element.505), channel_id=1, source_target_pairs={{1,0},{2,1},{3,2},{4,3},{5,4},{6,5},{7,6},{8,7},{9,8},{10,9},{11,1... | collective-permute-start | bytes 98312 | tf_op jit(solution)/shard_map/while/body/eval_jaxpr/ppermute | solution.py:10
  217.3 8.3 %collective-permute-start.2 = (bf16[256,64]{1,0:T(8,128)(2,1)S(1)}, bf16[256,64]{1,0:T(8,128)(2,1)S(1)}, u32[]{:S(2)}, u32[]{:S(2)}) collective-permute-start(bf16[256,64]{1,0:T(8,128)(2,1)S(1)} %get-tuple-element.505), channel_id=1, source_target_pairs={{1,0},{2,1},{3,2},{4,3},{5,4},{6,5},{7,6},{8,7},{9,8},{10,9},{11,1... | collective-permute-start | bytes 98312 | tf_op jit(solution)/shard_map/while/body/eval_jaxpr/ppermute | solution.py:10
  227.0 105.5 %psum.14 = f32[64,64]{0,1:T(8,128)S(1)} all-reduce(f32[64,64]{0,1:T(8,128)S(1)} %fusion.42), channel_id=1, replica_groups=mesh['grp'=16,'blk'=32] {'grp','blk'}, use_global_device_ids=true, to_apply=%region_5.6 | all-reduce | flops 4096 | bytes 32768 | tf_op jit(solution)/shard_map/psum | solution.py:28
  345.4 56.0 %while.49 = (s32[]{:T(128)}, f32[256,64]{0,1:T(8,128)S(1)}, bf16[256,64]{1,0:T(8,128)(2,1)S(1)}, s32[6]{0:T(128)S(1)}, bf16[6,256,256]{2,1,0:T(8,128)(2,1)S(1)}, /*index=5*/s32[]{:T(128)}) while((s32[]{:T(128)}, f32[256,64]{0,1:T(8,128)S(1)}, bf16[256,64]{1,0:T(8,128)(2,1)S(1)}, s32[6]{0:T(128)S(1)}, bf16[6,256,256]{2,1,0:T(8,128)(2,1)S(1)}, ...), condition=%wide.region_9.12_spmd, body=%wide.region_8.11_spmd.sunk | while | flops 9191432 | bytes 1409161 | solution.py:85
  382.5 8.3 %collective-permute-start.3 = (bf16[256,64]{1,0:T(8,128)(2,1)S(1)}, bf16[256,64]{1,0:T(8,128)(2,1)S(1)}, u32[]{:S(2)}, u32[]{:S(2)}) collective-permute-start(bf16[256,64]{1,0:T(8,128)(2,1)S(1)} %get-tuple-element.523), channel_id=1, source_target_pairs={{1,0},{2,1},{3,2},{4,3},{5,4},{6,5},{7,6},{8,7},{9,8},{10,9},{11,1... | collective-permute-start | bytes 98312 | tf_op jit(solution)/shard_map/while/body/eval_jaxpr/ppermute | solution.py:10
  392.0 8.3 %collective-permute-start.3 = (bf16[256,64]{1,0:T(8,128)(2,1)S(1)}, bf16[256,64]{1,0:T(8,128)(2,1)S(1)}, u32[]{:S(2)}, u32[]{:S(2)}) collective-permute-start(bf16[256,64]{1,0:T(8,128)(2,1)S(1)} %get-tuple-element.523), channel_id=1, source_target_pairs={{1,0},{2,1},{3,2},{4,3},{5,4},{6,5},{7,6},{8,7},{9,8},{10,9},{11,1... | collective-permute-start | bytes 98312 | tf_op jit(solution)/shard_map/while/body/eval_jaxpr/ppermute | solution.py:10
  401.6 103.1 %psum.15 = f32[64,64]{0,1:T(8,128)S(1)} all-reduce(f32[64,64]{0,1:T(8,128)S(1)} %fusion.43), channel_id=1, replica_groups=mesh['grp'=16,'blk'=32] {'grp','blk'}, use_global_device_ids=true, to_apply=%region_10.13 | all-reduce | flops 4096 | bytes 32768 | tf_op jit(solution)/shard_map/psum | solution.py:28
  (174 shorter events, 153.1 us)
Async XLA Ops:
  6.1 17.6 %collective-permute-start = (bf16[6,256,256]{2,1,0:T(8,128)(2,1)S(1)}, bf16[6,256,256]{2,1,0:T(8,128)(2,1)S(1)}, u32[]{:S(2)}, u32[]{:S(2)}) collective-permute-start(bf16[6,256,256]{2,1,0:T(8,128)(2,1)S(1)} %get-tuple-element.483), channel_id=1, source_target_pairs={{1,0},{2,1},{3,2},{4,3},{5,4},{6,5},{7,6},{8,7},{9,8},{10,9},{11,1... | collective-permute-start | bytes 2359304 | tf_op jit(solution)/shard_map/while/body/eval_jaxpr/ppermute | solution.py:10
  14.9 8.8 %collective-permute-start.1 = (bf16[6]{0:T(256)(128)(2,1)S(1)}, bf16[6]{0:T(256)(128)(2,1)S(1)}, u32[]{:S(2)}, u32[]{:S(2)}) collective-permute-start(bf16[6]{0:T(256)(128)(2,1)S(1)} %get-tuple-element.484), channel_id=1, source_target_pairs={{1,0},{2,1},{3,2},{4,3},{5,4},{6,5},{7,6},{8,7},{9,8},{10,9},{11,1... | collective-permute-start | bytes 44 | tf_op jit(solution)/shard_map/while/body/eval_jaxpr/ppermute | solution.py:10
  28.2 17.0 %collective-permute-start = (bf16[6,256,256]{2,1,0:T(8,128)(2,1)S(1)}, bf16[6,256,256]{2,1,0:T(8,128)(2,1)S(1)}, u32[]{:S(2)}, u32[]{:S(2)}) collective-permute-start(bf16[6,256,256]{2,1,0:T(8,128)(2,1)S(1)} %get-tuple-element.483), channel_id=1, source_target_pairs={{1,0},{2,1},{3,2},{4,3},{5,4},{6,5},{7,6},{8,7},{9,8},{10,9},{11,1... | collective-permute-start | bytes 2359304 | tf_op jit(solution)/shard_map/while/body/eval_jaxpr/ppermute | solution.py:10
  36.4 8.8 %collective-permute-start.1 = (bf16[6]{0:T(256)(128)(2,1)S(1)}, bf16[6]{0:T(256)(128)(2,1)S(1)}, u32[]{:S(2)}, u32[]{:S(2)}) collective-permute-start(bf16[6]{0:T(256)(128)(2,1)S(1)} %get-tuple-element.484), channel_id=1, source_target_pairs={{1,0},{2,1},{3,2},{4,3},{5,4},{6,5},{7,6},{8,7},{9,8},{10,9},{11,1... | collective-permute-start | bytes 44 | tf_op jit(solution)/shard_map/while/body/eval_jaxpr/ppermute | solution.py:10
  49.7 17.0 %collective-permute-start = (bf16[6,256,256]{2,1,0:T(8,128)(2,1)S(1)}, bf16[6,256,256]{2,1,0:T(8,128)(2,1)S(1)}, u32[]{:S(2)}, u32[]{:S(2)}) collective-permute-start(bf16[6,256,256]{2,1,0:T(8,128)(2,1)S(1)} %get-tuple-element.483), channel_id=1, source_target_pairs={{1,0},{2,1},{3,2},{4,3},{5,4},{6,5},{7,6},{8,7},{9,8},{10,9},{11,1... | collective-permute-start | bytes 2359304 | tf_op jit(solution)/shard_map/while/body/eval_jaxpr/ppermute | solution.py:10
  57.9 8.8 %collective-permute-start.1 = (bf16[6]{0:T(256)(128)(2,1)S(1)}, bf16[6]{0:T(256)(128)(2,1)S(1)}, u32[]{:S(2)}, u32[]{:S(2)}) collective-permute-start(bf16[6]{0:T(256)(128)(2,1)S(1)} %get-tuple-element.484), channel_id=1, source_target_pairs={{1,0},{2,1},{3,2},{4,3},{5,4},{6,5},{7,6},{8,7},{9,8},{10,9},{11,1... | collective-permute-start | bytes 44 | tf_op jit(solution)/shard_map/while/body/eval_jaxpr/ppermute | solution.py:10
  71.2 17.0 %collective-permute-start = (bf16[6,256,256]{2,1,0:T(8,128)(2,1)S(1)}, bf16[6,256,256]{2,1,0:T(8,128)(2,1)S(1)}, u32[]{:S(2)}, u32[]{:S(2)}) collective-permute-start(bf16[6,256,256]{2,1,0:T(8,128)(2,1)S(1)} %get-tuple-element.483), channel_id=1, source_target_pairs={{1,0},{2,1},{3,2},{4,3},{5,4},{6,5},{7,6},{8,7},{9,8},{10,9},{11,1... | collective-permute-start | bytes 2359304 | tf_op jit(solution)/shard_map/while/body/eval_jaxpr/ppermute | solution.py:10
  79.3 8.8 %collective-permute-start.1 = (bf16[6]{0:T(256)(128)(2,1)S(1)}, bf16[6]{0:T(256)(128)(2,1)S(1)}, u32[]{:S(2)}, u32[]{:S(2)}) collective-permute-start(bf16[6]{0:T(256)(128)(2,1)S(1)} %get-tuple-element.484), channel_id=1, source_target_pairs={{1,0},{2,1},{3,2},{4,3},{5,4},{6,5},{7,6},{8,7},{9,8},{10,9},{11,1... | collective-permute-start | bytes 44 | tf_op jit(solution)/shard_map/while/body/eval_jaxpr/ppermute | solution.py:10
  92.6 17.0 %collective-permute-start = (bf16[6,256,256]{2,1,0:T(8,128)(2,1)S(1)}, bf16[6,256,256]{2,1,0:T(8,128)(2,1)S(1)}, u32[]{:S(2)}, u32[]{:S(2)}) collective-permute-start(bf16[6,256,256]{2,1,0:T(8,128)(2,1)S(1)} %get-tuple-element.483), channel_id=1, source_target_pairs={{1,0},{2,1},{3,2},{4,3},{5,4},{6,5},{7,6},{8,7},{9,8},{10,9},{11,1... | collective-permute-start | bytes 2359304 | tf_op jit(solution)/shard_map/while/body/eval_jaxpr/ppermute | solution.py:10
  100.8 8.8 %collective-permute-start.1 = (bf16[6]{0:T(256)(128)(2,1)S(1)}, bf16[6]{0:T(256)(128)(2,1)S(1)}, u32[]{:S(2)}, u32[]{:S(2)}) collective-permute-start(bf16[6]{0:T(256)(128)(2,1)S(1)} %get-tuple-element.484), channel_id=1, source_target_pairs={{1,0},{2,1},{3,2},{4,3},{5,4},{6,5},{7,6},{8,7},{9,8},{10,9},{11,1... | collective-permute-start | bytes 44 | tf_op jit(solution)/shard_map/while/body/eval_jaxpr/ppermute | solution.py:10
  114.1 17.0 %collective-permute-start = (bf16[6,256,256]{2,1,0:T(8,128)(2,1)S(1)}, bf16[6,256,256]{2,1,0:T(8,128)(2,1)S(1)}, u32[]{:S(2)}, u32[]{:S(2)}) collective-permute-start(bf16[6,256,256]{2,1,0:T(8,128)(2,1)S(1)} %get-tuple-element.483), channel_id=1, source_target_pairs={{1,0},{2,1},{3,2},{4,3},{5,4},{6,5},{7,6},{8,7},{9,8},{10,9},{11,1... | collective-permute-start | bytes 2359304 | tf_op jit(solution)/shard_map/while/body/eval_jaxpr/ppermute | solution.py:10
  122.3 8.8 %collective-permute-start.1 = (bf16[6]{0:T(256)(128)(2,1)S(1)}, bf16[6]{0:T(256)(128)(2,1)S(1)}, u32[]{:S(2)}, u32[]{:S(2)}) collective-permute-start(bf16[6]{0:T(256)(128)(2,1)S(1)} %get-tuple-element.484), channel_id=1, source_target_pairs={{1,0},{2,1},{3,2},{4,3},{5,4},{6,5},{7,6},{8,7},{9,8},{10,9},{11,1... | collective-permute-start | bytes 44 | tf_op jit(solution)/shard_map/while/body/eval_jaxpr/ppermute | solution.py:10
  135.6 17.0 %collective-permute-start = (bf16[6,256,256]{2,1,0:T(8,128)(2,1)S(1)}, bf16[6,256,256]{2,1,0:T(8,128)(2,1)S(1)}, u32[]{:S(2)}, u32[]{:S(2)}) collective-permute-start(bf16[6,256,256]{2,1,0:T(8,128)(2,1)S(1)} %get-tuple-element.483), channel_id=1, source_target_pairs={{1,0},{2,1},{3,2},{4,3},{5,4},{6,5},{7,6},{8,7},{9,8},{10,9},{11,1... | collective-permute-start | bytes 2359304 | tf_op jit(solution)/shard_map/while/body/eval_jaxpr/ppermute | solution.py:10
  143.8 8.8 %collective-permute-start.1 = (bf16[6]{0:T(256)(128)(2,1)S(1)}, bf16[6]{0:T(256)(128)(2,1)S(1)}, u32[]{:S(2)}, u32[]{:S(2)}) collective-permute-start(bf16[6]{0:T(256)(128)(2,1)S(1)} %get-tuple-element.484), channel_id=1, source_target_pairs={{1,0},{2,1},{3,2},{4,3},{5,4},{6,5},{7,6},{8,7},{9,8},{10,9},{11,1... | collective-permute-start | bytes 44 | tf_op jit(solution)/shard_map/while/body/eval_jaxpr/ppermute | solution.py:10
  160.7 9.1 %collective-permute-start.2 = (bf16[256,64]{1,0:T(8,128)(2,1)S(1)}, bf16[256,64]{1,0:T(8,128)(2,1)S(1)}, u32[]{:S(2)}, u32[]{:S(2)}) collective-permute-start(bf16[256,64]{1,0:T(8,128)(2,1)S(1)} %get-tuple-element.505), channel_id=1, source_target_pairs={{1,0},{2,1},{3,2},{4,3},{5,4},{6,5},{7,6},{8,7},{9,8},{10,9},{11,1... | collective-permute-start | bytes 98312 | tf_op jit(solution)/shard_map/while/body/eval_jaxpr/ppermute | solution.py:10
  170.0 9.3 %collective-permute-start.2 = (bf16[256,64]{1,0:T(8,128)(2,1)S(1)}, bf16[256,64]{1,0:T(8,128)(2,1)S(1)}, u32[]{:S(2)}, u32[]{:S(2)}) collective-permute-start(bf16[256,64]{1,0:T(8,128)(2,1)S(1)} %get-tuple-element.505), channel_id=1, source_target_pairs={{1,0},{2,1},{3,2},{4,3},{5,4},{6,5},{7,6},{8,7},{9,8},{10,9},{11,1... | collective-permute-start | bytes 98312 | tf_op jit(solution)/shard_map/while/body/eval_jaxpr/ppermute | solution.py:10
  179.6 9.2 %collective-permute-start.2 = (bf16[256,64]{1,0:T(8,128)(2,1)S(1)}, bf16[256,64]{1,0:T(8,128)(2,1)S(1)}, u32[]{:S(2)}, u32[]{:S(2)}) collective-permute-start(bf16[256,64]{1,0:T(8,128)(2,1)S(1)} %get-tuple-element.505), channel_id=1, source_target_pairs={{1,0},{2,1},{3,2},{4,3},{5,4},{6,5},{7,6},{8,7},{9,8},{10,9},{11,1... | collective-permute-start | bytes 98312 | tf_op jit(solution)/shard_map/while/body/eval_jaxpr/ppermute | solution.py:10
  189.0 9.2 %collective-permute-start.2 = (bf16[256,64]{1,0:T(8,128)(2,1)S(1)}, bf16[256,64]{1,0:T(8,128)(2,1)S(1)}, u32[]{:S(2)}, u32[]{:S(2)}) collective-permute-start(bf16[256,64]{1,0:T(8,128)(2,1)S(1)} %get-tuple-element.505), channel_id=1, source_target_pairs={{1,0},{2,1},{3,2},{4,3},{5,4},{6,5},{7,6},{8,7},{9,8},{10,9},{11,1... | collective-permute-start | bytes 98312 | tf_op jit(solution)/shard_map/while/body/eval_jaxpr/ppermute | solution.py:10
  198.5 9.2 %collective-permute-start.2 = (bf16[256,64]{1,0:T(8,128)(2,1)S(1)}, bf16[256,64]{1,0:T(8,128)(2,1)S(1)}, u32[]{:S(2)}, u32[]{:S(2)}) collective-permute-start(bf16[256,64]{1,0:T(8,128)(2,1)S(1)} %get-tuple-element.505), channel_id=1, source_target_pairs={{1,0},{2,1},{3,2},{4,3},{5,4},{6,5},{7,6},{8,7},{9,8},{10,9},{11,1... | collective-permute-start | bytes 98312 | tf_op jit(solution)/shard_map/while/body/eval_jaxpr/ppermute | solution.py:10
  207.9 9.2 %collective-permute-start.2 = (bf16[256,64]{1,0:T(8,128)(2,1)S(1)}, bf16[256,64]{1,0:T(8,128)(2,1)S(1)}, u32[]{:S(2)}, u32[]{:S(2)}) collective-permute-start(bf16[256,64]{1,0:T(8,128)(2,1)S(1)} %get-tuple-element.505), channel_id=1, source_target_pairs={{1,0},{2,1},{3,2},{4,3},{5,4},{6,5},{7,6},{8,7},{9,8},{10,9},{11,1... | collective-permute-start | bytes 98312 | tf_op jit(solution)/shard_map/while/body/eval_jaxpr/ppermute | solution.py:10
  217.3 9.2 %collective-permute-start.2 = (bf16[256,64]{1,0:T(8,128)(2,1)S(1)}, bf16[256,64]{1,0:T(8,128)(2,1)S(1)}, u32[]{:S(2)}, u32[]{:S(2)}) collective-permute-start(bf16[256,64]{1,0:T(8,128)(2,1)S(1)} %get-tuple-element.505), channel_id=1, source_target_pairs={{1,0},{2,1},{3,2},{4,3},{5,4},{6,5},{7,6},{8,7},{9,8},{10,9},{11,1... | collective-permute-start | bytes 98312 | tf_op jit(solution)/shard_map/while/body/eval_jaxpr/ppermute | solution.py:10
  374.7 7.6 %collective-permute-start.3 = (bf16[256,64]{1,0:T(8,128)(2,1)S(1)}, bf16[256,64]{1,0:T(8,128)(2,1)S(1)}, u32[]{:S(2)}, u32[]{:S(2)}) collective-permute-start(bf16[256,64]{1,0:T(8,128)(2,1)S(1)} %get-tuple-element.523), channel_id=1, source_target_pairs={{1,0},{2,1},{3,2},{4,3},{5,4},{6,5},{7,6},{8,7},{9,8},{10,9},{11,1... | collective-permute-start | bytes 98312 | tf_op jit(solution)/shard_map/while/body/eval_jaxpr/ppermute | solution.py:10
  382.5 9.2 %collective-permute-start.3 = (bf16[256,64]{1,0:T(8,128)(2,1)S(1)}, bf16[256,64]{1,0:T(8,128)(2,1)S(1)}, u32[]{:S(2)}, u32[]{:S(2)}) collective-permute-start(bf16[256,64]{1,0:T(8,128)(2,1)S(1)} %get-tuple-element.523), channel_id=1, source_target_pairs={{1,0},{2,1},{3,2},{4,3},{5,4},{6,5},{7,6},{8,7},{9,8},{10,9},{11,1... | collective-permute-start | bytes 98312 | tf_op jit(solution)/shard_map/while/body/eval_jaxpr/ppermute | solution.py:10
  392.0 9.2 %collective-permute-start.3 = (bf16[256,64]{1,0:T(8,128)(2,1)S(1)}, bf16[256,64]{1,0:T(8,128)(2,1)S(1)}, u32[]{:S(2)}, u32[]{:S(2)}) collective-permute-start(bf16[256,64]{1,0:T(8,128)(2,1)S(1)} %get-tuple-element.523), channel_id=1, source_target_pairs={{1,0},{2,1},{3,2},{4,3},{5,4},{6,5},{7,6},{8,7},{9,8},{10,9},{11,1... | collective-permute-start | bytes 98312 | tf_op jit(solution)/shard_map/while/body/eval_jaxpr/ppermute | solution.py:10
  (8 other events, 34.6 us)
where the time goes:
time: 519 us; the launch traced here: 518 us
  blocking collectives  209 us (40%)
  starting transfers between devices  203 us (39%)
  matrix products  51.8 us (10%)
  other arithmetic  27.2 us (5%)
  waiting for transfers between devices  16.9 us (3%)
  local copies, waits for them, and re-layouts  8.97 us (2%)
    psum x2, blocking collectives, orthonormal(): gram_matrix = lax.psum(local_gram, ('grp', 'blk')) / total_nodes  209 us
    ppermute x28, starting transfers between devices, from_behind(): return lax.ppermute(block, axis, route)  203 us
    dot_general x8, matrix products, absorb(): jnp.einsum('ij,ajk->aik', left, right, preferred_element_type=jnp.float32)  23 us
    ppermute x28, waiting for transfers between devices, from_behind(): return lax.ppermute(block, axis, route)  16.9 us
    another operation x6, other arithmetic, orthonormal(): factor_lower = jnp.linalg.cholesky(gram_matrix)  13.1 us
    another operation x4, other arithmetic, orthonormal(): jax.scipy.linalg.solve_triangular(factor_lower, image.T, lower=True)  11.1 us
  transfers between devices with their start and end apart: 28, of which 14 were waited for; matrix products, arithmetic and copies ran while one was open for 3% of the time, Pallas kernels for 0%

commit v1 on v0

v1 whole, which is shorter than its diff:
```python
import jax
import jax.numpy as jnp
from jax import lax
from jax.experimental import pallas as pl
from jax.experimental.pallas import tpu as pltpu
from jax.sharding import PartitionSpec as P

TILE = 256
VEC = 64
SLOTS = 6
REACH = 8
NODES = 131072
BLK = 32
CHIPS = 16
NX, NY, NZ = 4, 8, 8
HALF = 16
F32 = jnp.float32
BF16 = jnp.bfloat16
NEED = [min(SLOTS, REACH - d) for d in range(REACH)]
SHIP = {1: 6, 2: 5, 3: 3}
ROWS = {1: 6, 2: 6, 3: 5, 4: 5, 5: 3, 6: 3, 7: 1}
NT = (((1,), (1,)), ((), ()))


def power_of_two(e):
    one = jnp.float32(1.0)
    return jnp.where(
        e == -2, 0.25 * one,
        jnp.where(e == -1, 0.5 * one, jnp.where(e == 0, one, jnp.where(e == 1, 2 * one, 4 * one))),
    )


def dot32(a, b, dims=(((1,), (0,)), ((), ()))):
    return lax.dot_general(
        a, b, dims, precision=lax.Precision.HIGHEST, preferred_element_type=F32
    )


def eliminate(blocks, first, last):
    blocks = list(blocks)
    sub = lax.broadcasted_iota(jnp.int32, (8, 128), 0)
    for k in range(first, last):
        kb, kr = divmod(k, 8)
        pivot_row = blocks[kb][kr : kr + 1, :]
        inverse = 1.0 / pivot_row[:, k : k + 1]
        row = pivot_row * inverse
        for i in range(kb, 8):
            factor = blocks[i][:, k : k + 1]
            if i == kb:
                if kr == 7:
                    continue
                factor = jnp.where(sub[:, :1] > kr, factor, 0.0)
            blocks[i] = blocks[i] - factor * row
    return blocks


def finish(blocks):
    lane = lax.broadcasted_iota(jnp.int32, (8, 128), 1)
    sub = lax.broadcasted_iota(jnp.int32, (8, 128), 0)
    done = []
    for i, block in enumerate(blocks):
        pivot = jnp.sum(jnp.where(lane == sub + 8 * i, block, 0.0), axis=1, keepdims=True)
        done.append(block * lax.rsqrt(pivot))
    return jnp.concatenate(done, axis=0)


def kernel(
    tv, off, ex, v0, out,
    own, rb1, rb2, rb3, rb4, rb5, rb6, rb7, meta, smeta, paths, motif, xs1, xs2,
    g_src, ga, gb_src, gb, gc_src, gc, gd_src, gd, fin,
    own_sem, smeta_sem, ts, tr, ms, mr, x1s, x1r, x2s, x2r,
    gas, gar, gbs, gbr, gcs, gcr, gds, gdr, ges, ger,
):
    rb = {1: rb1, 2: rb2, 3: rb3, 4: rb4, 5: rb5, 6: rb6, 7: rb7}
    g = lax.axis_index("grp")
    b = lax.axis_index("blk")
    c = lax.rem(b, 2)
    q = b // 2
    x_hi, z = lax.rem(q, 2), q // 2
    x_lo, y = lax.rem(g, 2), g // 2
    x = x_hi * 2 + x_lo

    def at_blk(chip, core):
        return {"grp": g, "blk": lax.rem(chip + 2 * CHIPS, CHIPS) * 2 + core}

    def at_behind(d):
        return {"grp": g, "blk": lax.rem(b + BLK - d, BLK)}

    def at_xyz(xx, yy, zz):
        return {
            "grp": yy * 2 + lax.rem(xx, 2),
            "blk": (zz * 2 + xx // 2) * 2 + c,
        }

    sibling = at_blk(q, 1 - c)
    cross = at_blk(q - 4 + 8 * c, 1 - c)
    x_mates = [at_xyz(lax.rem(x + j, NX), y, z) for j in range(1, NX)]
    y_mates = [at_xyz(x, lax.rem(y + j, NY), z) for j in range(1, NY)]
    z_mates = [at_xyz(x, y, lax.rem(z + j, NZ)) for j in range(1, NZ)]

    def remote(src, dst, ssem, rsem, dev):
        return pltpu.make_async_remote_copy(
            src_ref=src, dst_ref=dst, send_sem=ssem, recv_sem=rsem,
            device_id=dev, device_id_type=pl.DeviceIdType.MESH,
        )

    load_own = pltpu.make_async_copy(tv.at[0], own, own_sem)
    load_own.start()

    offs = [off[0, s] for s in range(SLOTS)]
    exps = [ex[0, s] for s in range(SLOTS)]
    lane8 = lax.broadcasted_iota(jnp.int32, (8, 128), 1)
    note = jnp.zeros((8, 128), jnp.int32)
    for s in range(SLOTS):
        note = jnp.where(lane8 == s, offs[s], note)
        note = jnp.where(lane8 == 8 + s, exps[s], note)
    meta[0] = note

    barrier = pltpu.get_barrier_semaphore()
    met = x_mates + y_mates + z_mates
    for d in range(1, REACH):
        met.append(at_behind(d))
        met.append(at_behind(-d))
    for dev in met:
        pl.semaphore_signal(barrier, inc=1, device_id=dev, device_id_type=pl.DeviceIdType.MESH)
    pl.semaphore_wait(barrier, len(met))

    tile_out = [
        remote(tv.at[0, pl.ds(0, n)], rb[2 * k].at[pl.ds(0, n)], ts.at[k], tr.at[2 * k], at_blk(q - k, c))
        for k, n in SHIP.items()
    ]
    far_tile = remote(tv.at[0, pl.ds(0, 1)], rb[7], ts.at[4], tr.at[7], cross)
    near_tile = remote(tv.at[0], rb[1], ts.at[5], tr.at[1], sibling)
    note_out = [
        remote(meta.at[0], meta.at[d], ms.at[d], mr.at[d], at_behind(d)) for d in range(1, REACH)
    ]
    for copy in note_out:
        copy.start()
    for copy in tile_out:
        copy.start()

    @pl.when(c == 0)
    def _():
        far_tile.start()

    @pl.when(c == 1)
    def _():
        near_tile.start()

    load_own.wait()

    def hand_on(k):
        copies = []
        for core in range(2):
            d = 2 * k - 1 + 2 * core
            copies.append(
                remote(rb[2 * k].at[pl.ds(0, NEED[d])], rb[d], ts.at[5 + k], tr.at[d], sibling)
            )
        return copies

    def by_core(copies, act):
        for core in range(2):
            @pl.when(c == core)
            def _(copy=copies[core]):
                act(copy)

    def absorb(d, right_ref, first):
        slot = jnp.int32(0)
        grade = jnp.float32(0.0)
        for r in range(SLOTS):
            hit = offs[r] == d
            slot = jnp.where(hit, r, slot)
            grade = jnp.where(hit, power_of_two(exps[r]), grade)
        left = own[slot]

        def one(s, carry):
            wanted = smeta[0, 0, s] - d
            t = jnp.int32(0)
            scale = jnp.float32(0.0)
            for j in range(NEED[d]):
                hit = smeta[d, 0, j] == wanted
                t = jnp.where(hit, j, t)
                scale = jnp.where(hit, power_of_two(smeta[d, 0, 8 + j]), scale)
            product = jnp.dot(left, right_ref[t], preferred_element_type=F32) * (grade * scale)
            if first:
                paths[s] = product
            else:
                paths[s] = paths[s] + product
            return carry

        lax.fori_loop(0 if d == 0 else max(1, d - 2), SLOTS, one, 0)

    for copy in note_out:
        copy.wait_recv()
    to_scalar = pltpu.make_async_copy(meta, smeta, smeta_sem)
    to_scalar.start()
    to_scalar.wait()

    absorb(0, own, True)
    for k in range(1, 4):
        tile_out[k - 1].wait_recv()
        by_core(hand_on(k), lambda copy: copy.start())
        absorb(2 * k, rb[2 * k], False)
        d = 2 * k - 1
        remote(rb[d], rb[d], ts.at[0], tr.at[d], sibling).wait_recv()
        absorb(d, rb[d], False)
    remote(rb[7], rb[7], ts.at[0], tr.at[7], sibling).wait_recv()
    absorb(7, rb[7], False)

    ones = jnp.ones((8, TILE), BF16)
    degree = jnp.zeros((8, TILE), F32)
    for s in range(SLOTS):
        tile = ((own[s].astype(F32) * power_of_two(exps[s])) * paths[s]).astype(BF16)
        motif[s] = tile
        degree = degree + lax.dot_general(ones, tile, NT, preferred_element_type=F32)
    degree = degree[0:1, :]
    root = lax.rsqrt(degree)

    def exchange(xs, ssem, rsem):
        direct = [remote(xs.at[0], xs.at[2 * k], ssem.at[k], rsem.at[2 * k], at_blk(q - k, c)) for k in (1, 2, 3)]
        far = remote(xs.at[0], xs.at[7], ssem.at[4], rsem.at[7], cross)
        near = remote(xs.at[0], xs.at[1], ssem.at[5], rsem.at[1], sibling)

        @pl.when(c == 0)
        def _():
            far.start()

        @pl.when(c == 1)
        def _():
            near.start()

        for copy in direct:
            copy.start()
        return direct, far, near

    def passing(xs, ssem, rsem, k):
        return [
            remote(xs.at[2 * k], xs.at[2 * k - 1 + 2 * core], ssem.at[5 + k], rsem.at[2 * k - 1 + 2 * core], sibling)
            for core in range(2)
        ]

    def relay(xs, ssem, rsem, direct):
        for k in (1, 2, 3):
            direct[k - 1].wait_recv()
            by_core(passing(xs, ssem, rsem, k), lambda copy: copy.start())
        for d in (1, 3, 5, 7):
            remote(xs.at[d], xs.at[d], ssem.at[0], rsem.at[d], sibling).wait_recv()

    def apply_graph(xs):
        total = jnp.zeros((VEC, TILE), F32)
        for s in range(SLOTS):
            total = total + lax.dot_general(xs[offs[s]], motif[s], NT, preferred_element_type=F32)
        return total

    lane = lax.broadcasted_iota(jnp.int32, (64, 128), 1)
    row = lax.broadcasted_iota(jnp.int32, (64, 128), 0)
    left = lane < VEC
    zeros = jnp.zeros((64, 128), F32)

    def gram(i, vectors):
        both = dot32(vectors, jnp.concatenate([vectors, vectors], axis=0), NT)
        g_src[i] = jnp.where(left[:32], both[:32], both[32:]) / NODES

    def copies_a(i):
        return [remote(g_src.at[i, pl.ds((1 - c) * HALF, HALF)], ga.at[i], gas.at[i], gar.at[i], sibling)]

    def copies_b(i):
        return [remote(gb_src.at[i], gb.at[i, j], gbs.at[i, j], gbr.at[i, j], x_mates[j]) for j in range(NX - 1)]

    def copies_c(i):
        return [remote(gc_src.at[i], gc.at[i, j], gcs.at[i, j], gcr.at[i, j], y_mates[j]) for j in range(NY - 1)]

    def copies_d(i):
        return [remote(gd_src.at[i], gd.at[i, j], gds.at[i, j], gdr.at[i, j], z_mates[j]) for j in range(NZ - 1)]

    def copies_e(i):
        mine = pl.ds(c * HALF, HALF)
        return [remote(fin.at[i, mine], fin.at[i, mine], ges.at[i], ger.at[i], sibling)]

    def start(copies):
        for copy in copies:
            copy.start()

    def arrive(copies):
        for copy in copies:
            copy.wait_recv()

    def step_a(i):
        start(copies_a(i))

    def step_b(i):
        arrive(copies_a(i))
        gb_src[i] = g_src[i, pl.ds(c * HALF, HALF), :] + ga[i]
        start(copies_b(i))

    def step_c(i):
        arrive(copies_b(i))
        gc_src[i] = gb_src[i] + (gb[i, 0] + gb[i, 1] + gb[i, 2])
        start(copies_c(i))

    def step_d(i):
        arrive(copies_c(i))
        gd_src[i] = gc_src[i] + sum(gc[i, j] for j in range(1, 7)) + gc[i, 0]
        start(copies_d(i))

    def step_e(i):
        arrive(copies_d(i))
        fin[i, pl.ds(c * HALF, HALF), :] = gd_src[i] + sum(gd[i, j] for j in range(1, 7)) + gd[i, 0]
        start(copies_e(i))

    def collect(i):
        other = pl.ds((1 - c) * HALF, HALF)
        remote(fin.at[i, other], fin.at[i, other], ges.at[i], ger.at[i], sibling).wait_recv()
        packed = fin[i]
        turned = pltpu.roll(packed, 64, 1)
        return jnp.concatenate(
            [jnp.where(left[:32], packed, turned), jnp.where(left[:32], turned, packed)], axis=0
        )

    unit = (
        lax.broadcasted_iota(jnp.int32, (VEC, VEC), 0) == lax.broadcasted_iota(jnp.int32, (VEC, VEC), 1)
    ).astype(BF16)
    start_t = lax.dot_general(unit, v0[...], NT, preferred_element_type=F32)
    input_1 = (start_t * root).astype(BF16)
    xs1[0] = input_1
    sent_1 = exchange(xs1, x1s, x1r)
    relay(xs1, x1s, x1r, sent_1[0])
    scaled_1 = (apply_graph(xs1) + degree * input_1.astype(F32)) * root

    wide_2 = scaled_1 * root
    xs2[0] = wide_2.astype(BF16)
    sent_2 = exchange(xs2, x2s, x2r)
    gram(0, scaled_1)
    step_a(0)
    step_b(0)
    relay(xs2, x2s, x2r, sent_2[0])
    step_c(0)
    scaled_2 = (apply_graph(xs2) + degree * wide_2) * root
    gram(1, scaled_2)
    step_a(1)
    step_d(0)
    step_b(1)
    step_e(0)
    gram_1 = collect(0)
    step_c(1)
    augmented = jnp.where(left, gram_1, jnp.where(lane == row + VEC, 1.0, 0.0))
    blocks = [augmented[8 * i : 8 * i + 8] for i in range(8)]
    blocks = eliminate(blocks, 0, 24)
    step_d(1)
    blocks = eliminate(blocks, 24, VEC)
    inverse_1 = jnp.where(left, 0.0, finish(blocks))
    step_e(1)
    gram_2 = jnp.where(left, 0.0, collect(1))
    half_way = dot32(inverse_1, jnp.concatenate([zeros, gram_2], axis=0))
    middle = dot32(half_way, jnp.concatenate([inverse_1, zeros], axis=0), NT)
    augmented = jnp.where(left, middle, inverse_1)
    blocks = eliminate([augmented[8 * i : 8 * i + 8] for i in range(8)], 0, VEC)
    inverse_2 = jnp.where(left, 0.0, finish(blocks))
    out[...] = dot32(inverse_2, jnp.concatenate([jnp.zeros((VEC, TILE), F32), scaled_2], axis=0))

    for copy in note_out + tile_out + sent_1[0] + sent_2[0]:
        copy.wait_send()

    @pl.when(c == 0)
    def _():
        far_tile.wait_send()
        sent_1[1].wait_send()
        sent_2[1].wait_send()

    @pl.when(c == 1)
    def _():
        near_tile.wait_send()
        sent_1[2].wait_send()
        sent_2[2].wait_send()

    for k in (1, 2, 3):
        by_core(hand_on(k), lambda copy: copy.wait_send())
        by_core(passing(xs1, x1s, x1r, k), lambda copy: copy.wait_send())
        by_core(passing(xs2, x2s, x2r, k), lambda copy: copy.wait_send())
    for i in range(2):
        for copies in (copies_a, copies_b, copies_c, copies_d, copies_e):
            for copy in copies(i):
                copy.wait_send()


def shards(tile_values, tile_offset, tile_exponent, initial_vectors):
    dma = pltpu.SemaphoreType.DMA
    tiles = [pltpu.VMEM((ROWS[d], TILE, TILE), BF16) for d in range(1, REACH)]
    basis_t = pl.pallas_call(
        kernel,
        out_shape=jax.ShapeDtypeStruct((VEC, TILE), F32),
        in_specs=[
            pl.BlockSpec(memory_space=pl.ANY),
            pl.BlockSpec(memory_space=pltpu.SMEM),
            pl.BlockSpec(memory_space=pltpu.SMEM),
            pl.BlockSpec(memory_space=pltpu.VMEM),
        ],
        out_specs=pl.BlockSpec(memory_space=pltpu.VMEM),
        scratch_shapes=[
            pltpu.VMEM((SLOTS, TILE, TILE), BF16),
            *tiles,
            pltpu.VMEM((REACH, 8, 128), jnp.int32),
            pltpu.SMEM((REACH, 8, 128), jnp.int32),
            pltpu.VMEM((SLOTS, TILE, TILE), F32),
            pltpu.VMEM((SLOTS, TILE, TILE), BF16),
            pltpu.VMEM((REACH, VEC, TILE), BF16),
            pltpu.VMEM((REACH, VEC, TILE), BF16),
            pltpu.VMEM((2, 2 * HALF, 128), F32),
            pltpu.VMEM((2, HALF, 128), F32),
            pltpu.VMEM((2, HALF, 128), F32),
            pltpu.VMEM((2, NX - 1, HALF, 128), F32),
            pltpu.VMEM((2, HALF, 128), F32),
            pltpu.VMEM((2, NY - 1, HALF, 128), F32),
            pltpu.VMEM((2, HALF, 128), F32),
            pltpu.VMEM((2, NZ - 1, HALF, 128), F32),
            pltpu.VMEM((2, 2 * HALF, 128), F32),
            dma, dma,
            dma((9,)), dma((8,)),
            dma((8,)), dma((8,)),
            dma((9,)), dma((8,)),
            dma((9,)), dma((8,)),
            dma((2,)), dma((2,)),
            dma((2, NX - 1)), dma((2, NX - 1)),
            dma((2, NY - 1)), dma((2, NY - 1)),
            dma((2, NZ - 1)), dma((2, NZ - 1)),
            dma((2,)), dma((2,)),
        ],
        compiler_params=pltpu.CompilerParams(
            collective_id=0, has_side_effects=True, vmem_limit_bytes=40 * 1024 * 1024
        ),
        cost_estimate=pl.CostEstimate(flops=1200000000, bytes_accessed=1000000, transcendentals=0),
        name="embed",
    )(tile_values, tile_offset, tile_exponent, initial_vectors)
    return basis_t.T


def solution(mesh):
    return jax.shard_map(
        shards,
        mesh=mesh,
        in_specs=(
            P(("grp", "blk"), None, None, None),
            P(("grp", "blk"), None),
            P(("grp", "blk"), None),
            P(("grp", "blk"), None),
        ),
        out_specs=P(("grp", "blk"), None),
        check_vma=False,
    )
```

time: 519 us -> 121 us (0.23)
  blocking collectives: 209 us -> 0 us
  starting transfers between devices: 203 us -> 0 us
  Pallas kernels: 0 us -> 118 us
  matrix products: 51.8 us -> 0 us
  other arithmetic: 27.2 us -> 0 us
  waiting for transfers between devices: 16.9 us -> 0 us
  local copies, waits for them, and re-layouts: 8.97 us -> 2.66 us
    psum x2 -> x0, blocking collectives: 209 us -> none  [orthonormal(): gram_matrix = lax.psum(local_gram, ('grp', 'blk')) / total_nodes]
    ppermute x28 -> x0, starting transfers between devices: 203 us -> none  [from_behind(): return lax.ppermute(block, axis, route)]
    pallas_call x0 -> x1, Pallas kernels: none -> 118 us  [shards(): pl.pallas_call(kernel, out_shape=jax.ShapeDtypeStruct((VEC, TILE), F32),...]
    dot_general x57 -> x0, matrix products: 50.7 us -> none  [the longest x8 23 us: absorb(): jnp.einsum('ij,ajk->aik', left, right, preferred_element_type=jnp.float32)]
    another operation x10 -> x0, other arithmetic: 24.3 us -> none  [the longest x6 13.1 us: orthonormal(): factor_lower = jnp.linalg.cholesky(gram_matrix)]
    ppermute x28 -> x0, waiting for transfers between devices: 16.9 us -> none  [from_behind(): return lax.ppermute(block, axis, route)]
    dot_general x8 -> x0, local copies, waits for them, and re-layouts: 5.72 us -> none  [absorb(): jnp.einsum('ac,cij->aij', meets.astype(jnp.bfloat16), values, preferred_e...]
  transfers between devices with their start and end apart: 28 -> 0, of which waited for: 14 -> 0; matrix products, arithmetic and copies ran while one was open for 3% -> 0% of each run, Pallas kernels for 0% -> 0%
where the time goes in v1:
time: 121 us
  Pallas kernels  118 us (98%)
  local copies, waits for them, and re-layouts  2.66 us (2%)
    pallas_call x1, Pallas kernels, shards(): pl.pallas_call(kernel, out_shape=jax.ShapeDtypeStruct((VEC, TILE), F32),...  118 us
    unnamed x8, local copies, waits for them, and re-layouts  2.66 us

profile of v1, /device:TPU:1, one launch (start us, length us, event | category | flops | bytes accessed | tf_op | source)
XLA Modules:
  0.0 120.6 jit_solution(12395323386843314781)
XLA Ops:
  0.0 0.0 copy-start.2
  0.0 0.0 copy-start.1
  0.0 0.9 copy.5.v0
  0.9 0.0 copy-done.2
  0.9 0.0 copy-done.1
  0.9 0.0 copy-start
  0.9 1.1 copy-done
  2.1 117.9 %embed.1 = f32[64,256]{1,0:T(8,128)S(1)} custom-call(bf16[1,6,256,256]{3,2,1,0:T(8,128)(2,1)S(1)} %copy-done, s32[1,6]{1,0:T(1,128)S(1)} %copy-done.1, s32[1,6]{1,0:T(1,128)S(1)} %copy-done.2, bf16[256,64]{1,0:T(8,128)(2,1)S(1)} %copy.5.v0), custom_call_target="tpu_custom_call" | custom-call | flops 1200000000 | bytes 1000000 | tf_op jit(solution)/shard_map/embed/pallas_call | solution.py:389
  120.0 0.6 copy.7
Async XLA Ops:
  0.0 0.9 copy-start.2
  0.0 0.9 copy-start.1
  0.9 1.1 copy-start

commit v2 on v1

v2 whole, which is shorter than its diff:
```python
import jax
import jax.numpy as jnp
from jax import lax
from jax.experimental import pallas as pl
from jax.experimental.pallas import tpu as pltpu
from jax.sharding import PartitionSpec as P

TILE = 256
VEC = 64
SLOTS = 6
REACH = 8
NODES = 131072
BLK = 32
CHIPS = 16
NX, NY, NZ = 4, 8, 8
HALF = 16
F32 = jnp.float32
BF16 = jnp.bfloat16
NEED = [min(SLOTS, REACH - d) for d in range(REACH)]
PIECES = [(0, 1), (1, 3), (3, 5), (5, 6)]
PARTS = {1: [(0, 3), (3, 6)], 3: [(0, 3), (3, 5)], 5: [(0, 3)], 7: [(0, 1)]}
ROWS = {1: 6, 2: 6, 3: 5, 4: 6, 5: 3, 6: 3, 7: 1}
NT = (((1,), (1,)), ((), ()))


def power_of_two(e):
    one = jnp.float32(1.0)
    return jnp.where(
        e == -2, 0.25 * one,
        jnp.where(e == -1, 0.5 * one, jnp.where(e == 0, one, jnp.where(e == 1, 2 * one, 4 * one))),
    )


def dot32(a, b, dims=(((1,), (0,)), ((), ()))):
    return lax.dot_general(
        a, b, dims, precision=lax.Precision.HIGHEST, preferred_element_type=F32
    )


def eliminate(blocks, first, last):
    blocks = list(blocks)
    sub = lax.broadcasted_iota(jnp.int32, (8, 128), 0)

    def spread(row):
        return jnp.broadcast_to(row, (8, 128))

    for k in range(first, last, 4):
        kb, kr = divmod(k, 8)
        head = blocks[kb]
        columns = {
            i: [spread(blocks[i][:, k + j : k + j + 1]) for j in range(4)]
            for i in range(kb, 8)
        }
        upper = [spread(head[kr + j : kr + j + 1, :]) for j in range(4)]
        corner = [[spread(columns[kb][j][kr + a : kr + a + 1, :]) for j in range(4)] for a in range(4)]
        inverse = []
        for a in range(4):
            inverse.append(1.0 / corner[a][a])
            for r in range(a + 1, 4):
                low = corner[a][r] * inverse[a]
                for j in range(r, 4):
                    corner[r][j] = corner[r][j] - low * corner[a][j]
                upper[r] = upper[r] - low * upper[a]
        for i in range(kb, 8):
            if i == kb and kr == 4:
                continue
            block = blocks[i]
            factors = []
            for a in range(4):
                rest = columns[i][a]
                for e in range(a):
                    rest = rest - factors[e] * corner[e][a]
                factors.append(rest * inverse[a])
            for a in range(4):
                block = block - factors[a] * upper[a]
            blocks[i] = block if i > kb else jnp.where(sub > kr + 3, block, head)
        done = blocks[kb]
        for a in range(4):
            done = jnp.where(sub == kr + a, upper[a], done)
        blocks[kb] = done
    return blocks


def finish(blocks):
    lane = lax.broadcasted_iota(jnp.int32, (8, 128), 1)
    sub = lax.broadcasted_iota(jnp.int32, (8, 128), 0)
    done = []
    for i, block in enumerate(blocks):
        pivot = jnp.sum(jnp.where(lane == sub + 8 * i, block, 0.0), axis=1, keepdims=True)
        done.append(block * lax.rsqrt(pivot))
    return jnp.concatenate(done, axis=0)


def kernel(
    tv, off_any, ex_any, v0, out,
    own, rb1, rb2, rb3, rb4, rb5, rb6, rb7, off, ex, meta, smeta, paths, motif, xs1, xs2,
    g_src, gb, gc_src, gc, gd_src, gd, fin,
    own_sem, in_sem, smeta_sem, ts, tr, ms, mr, x1s, x1r, x2s, x2r,
    gbs, gbr, gcs, gcr, gds, gdr, ges, ger,
):
    rb = {1: rb1, 2: rb2, 3: rb3, 4: rb4, 5: rb5, 6: rb6, 7: rb7}
    g = lax.axis_index("grp")
    b = lax.axis_index("blk")
    c = lax.rem(b, 2)
    q = b // 2
    x_hi, z = lax.rem(q, 2), q // 2
    x_lo, y = lax.rem(g, 2), g // 2
    x = x_hi * 2 + x_lo

    def at_blk(chip, core):
        return {"grp": g, "blk": lax.rem(chip + 2 * CHIPS, CHIPS) * 2 + core}

    def at_behind(d):
        return {"grp": g, "blk": lax.rem(b + BLK - d, BLK)}

    def at_xyz(xx, yy, zz, core=c):
        return {
            "grp": yy * 2 + lax.rem(xx, 2),
            "blk": (zz * 2 + xx // 2) * 2 + core,
        }

    sibling = at_blk(q, 1 - c)
    cross = at_blk(q - 4 + 8 * c, 1 - c)
    facing = at_blk(q + 1 - 2 * x_hi, c)
    below = at_blk(q - 2, c)
    x_mates = [at_xyz(lax.rem(x + j, NX), y, z) for j in range(1, NX)]
    x_others = [at_xyz(lax.rem(x + j, NX), y, z, 1 - c) for j in range(NX)]
    y_mates = [at_xyz(x, lax.rem(y + j, NY), z) for j in range(1, NY)]
    z_mates = [at_xyz(x, y, lax.rem(z + j, NZ)) for j in range(1, NZ)]

    def remote(src, dst, ssem, rsem, dev):
        return pltpu.make_async_remote_copy(
            src_ref=src, dst_ref=dst, send_sem=ssem, recv_sem=rsem,
            device_id=dev, device_id_type=pl.DeviceIdType.MESH,
        )

    load_own = pltpu.make_async_copy(tv.at[0], own, own_sem)
    load_own.start()
    load_off = pltpu.make_async_copy(off_any, off, in_sem.at[0])
    load_ex = pltpu.make_async_copy(ex_any, ex, in_sem.at[1])
    load_off.start()
    load_ex.start()

    barrier = pltpu.get_barrier_semaphore()
    met = x_mates + x_others[1:] + y_mates + z_mates
    for d in range(1, REACH):
        met.append(at_behind(d))
        met.append(at_behind(-d))
    for dev in met:
        pl.semaphore_signal(barrier, inc=1, device_id=dev, device_id_type=pl.DeviceIdType.MESH)
    load_off.wait()
    load_ex.wait()
    offs = [off[0, s] for s in range(SLOTS)]
    exps = [ex[0, s] for s in range(SLOTS)]
    lane8 = lax.broadcasted_iota(jnp.int32, (8, 128), 1)
    note = jnp.zeros((8, 128), jnp.int32)
    for s in range(SLOTS):
        note = jnp.where(lane8 == s, offs[s], note)
        note = jnp.where(lane8 == 8 + s, exps[s], note)
    meta[0] = note
    pl.semaphore_wait(barrier, len(met))

    def piece(src, d, j, sem, dev):
        lo, hi = PIECES[j]
        return remote(src.at[pl.ds(lo, hi - lo)], rb[d].at[pl.ds(lo, hi - lo)], ts.at[sem + j], tr.at[d, j], dev)

    mine = tv.at[0]
    own_down = [piece(mine, 4, j, 0, below) for j in range(4)]
    own_facing = [piece(mine, 2, j, 4, facing) for j in range(4)]
    on_facing = [piece(rb4, 2, j, 4, facing) for j in range(4)]
    on_down = [piece(rb2, 6, j, 8, below) for j in range(2)]
    far_tile = remote(tv.at[0, pl.ds(0, 1)], rb7, ts.at[10], tr.at[7, 0], cross)

    def part(src, d, p, sem):
        lo, hi = PARTS[d][p]
        return remote(src.at[pl.ds(lo, hi - lo)], rb[d].at[pl.ds(lo, hi - lo)], ts.at[sem + p], tr.at[d, p], sibling)

    near_tiles = [part(mine, 1, p, 11) for p in range(2)]
    note_out = [
        remote(meta.at[0], meta.at[d], ms.at[d], mr.at[d], at_behind(d)) for d in range(1, REACH)
    ]
    even, odd = x_hi == 0, x_hi == 1
    for copy in note_out:
        copy.start()

    @pl.when(even)
    def _():
        for j in range(4):
            own_down[j].start()

    @pl.when(odd)
    def _():
        for j in range(4):
            own_facing[j].start()
            if j < 3:
                own_down[j].start()

    @pl.when(c == 1)
    def _():
        for copy in near_tiles:
            copy.start()

    @pl.when(c == 0)
    def _():
        far_tile.start()

    def hand_on(k, p):
        return [
            part(rb[2 * k], d, p, 11 + 2 * k) if p < len(PARTS[d]) else None
            for d in (2 * k - 1, 2 * k + 1)
        ]

    def by_core(copies, act):
        for core in range(2):
            if copies[core] is not None:
                @pl.when(c == core)
                def _(copy=copies[core]):
                    act(copy)

    def go(copy):
        copy.start()

    def left_here(copy):
        copy.wait_send()

    def here(d):
        for p in range(len(PARTS[d])):
            part(rb[d], d, p, 11).wait_recv()

    def absorb(d, right_ref, first):
        slot = jnp.int32(0)
        grade = jnp.float32(0.0)
        for r in range(SLOTS):
            hit = offs[r] == d
            slot = jnp.where(hit, r, slot)
            grade = jnp.where(hit, power_of_two(exps[r]), grade)
        left = own[slot]

        def one(s, carry):
            wanted = smeta[0, 0, s] - d
            t = jnp.int32(0)
            scale = jnp.float32(0.0)
            for j in range(NEED[d]):
                hit = smeta[d, 0, j] == wanted
                t = jnp.where(hit, j, t)
                scale = jnp.where(hit, power_of_two(smeta[d, 0, 8 + j]), scale)
            product = jnp.dot(left, right_ref[t], preferred_element_type=F32) * (grade * scale)
            if first:
                paths[s] = product
            else:
                paths[s] = paths[s] + product
            return carry

        lax.fori_loop(0 if d == 0 else max(1, d - 2), SLOTS, one, 0)

    for j in range(4):
        if j < 3:
            own_down[j].wait_recv()

        @pl.when(even)
        def _(j=j):
            if j == 3:
                own_down[j].wait_recv()
            on_facing[j].start()

        own_facing[j].wait_recv()
        if j < 2:
            on_down[j].start()
        if j == 1:
            by_core(hand_on(1, 0), go)
            by_core(hand_on(2, 0), go)
            for copy in note_out:
                copy.wait_recv()
            to_scalar = pltpu.make_async_copy(meta, smeta, smeta_sem)
            to_scalar.start()
            to_scalar.wait()
            load_own.wait()
            absorb(0, own, True)
        if j == 2:
            by_core(hand_on(2, 1), go)
    by_core(hand_on(1, 1), go)
    absorb(4, rb4, False)
    absorb(2, rb2, False)
    for j in range(2):
        on_down[j].wait_recv()
    by_core(hand_on(3, 0), go)
    absorb(6, rb6, False)
    for d in (1, 3, 5, 7):
        here(d)
        absorb(d, rb[d], False)

    ones = jnp.ones((8, TILE), BF16)
    degree = jnp.zeros((8, TILE), F32)
    for s in range(SLOTS):
        tile = ((own[s].astype(F32) * power_of_two(exps[s])) * paths[s]).astype(BF16)
        motif[s] = tile
        degree = degree + lax.dot_general(ones, tile, NT, preferred_element_type=F32)
    degree = degree[0:1, :]
    root = lax.rsqrt(degree)

    def exchange(xs, ssem, rsem):
        return [remote(xs.at[0], xs.at[d], ssem.at[d], rsem.at[d], at_behind(d)) for d in range(1, REACH)]

    def apply_graph(xs):
        total = jnp.zeros((VEC, TILE), F32)
        for s in range(SLOTS):
            total = total + lax.dot_general(xs[offs[s]], motif[s], NT, preferred_element_type=F32)
        return total

    lane = lax.broadcasted_iota(jnp.int32, (64, 128), 1)
    row = lax.broadcasted_iota(jnp.int32, (64, 128), 0)
    left = lane < VEC
    zeros = jnp.zeros((64, 128), F32)

    def gram(i, vectors):
        both = dot32(vectors, jnp.concatenate([vectors, vectors], axis=0), NT)
        g_src[i] = jnp.where(left[:32], both[:32], both[32:]) / NODES

    def copies_b(i):
        own_half, other_half = pl.ds(c * HALF, HALF), pl.ds((1 - c) * HALF, HALF)
        return [
            remote(g_src.at[i, other_half], gb.at[i, 3 + j], gbs.at[i, 3 + j], gbr.at[i, 3 + j], x_others[j])
            for j in range(NX)
        ] + [
            remote(g_src.at[i, own_half], gb.at[i, j], gbs.at[i, j], gbr.at[i, j], x_mates[j])
            for j in range(NX - 1)
        ]

    def copies_c(i):
        return [remote(gc_src.at[i], gc.at[i, j], gcs.at[i, j], gcr.at[i, j], y_mates[j]) for j in range(NY - 1)]

    def copies_d(i):
        return [remote(gd_src.at[i], gd.at[i, j], gds.at[i, j], gdr.at[i, j], z_mates[j]) for j in range(NZ - 1)]

    def copies_e(i):
        mine = pl.ds(c * HALF, HALF)
        return [remote(fin.at[i, mine], fin.at[i, mine], ges.at[i], ger.at[i], sibling)]

    def start(copies):
        for copy in copies:
            copy.start()

    def arrive(copies):
        for copy in copies:
            copy.wait_recv()

    def step_b(i):
        start(copies_b(i))

    def step_c(i):
        arrive(copies_b(i))
        gc_src[i] = g_src[i, pl.ds(c * HALF, HALF), :] + sum(gb[i, j] for j in range(1, 7)) + gb[i, 0]
        start(copies_c(i))

    def step_d(i):
        arrive(copies_c(i))
        gd_src[i] = gc_src[i] + sum(gc[i, j] for j in range(1, 7)) + gc[i, 0]
        start(copies_d(i))

    def step_e(i):
        arrive(copies_d(i))
        fin[i, pl.ds(c * HALF, HALF), :] = gd_src[i] + sum(gd[i, j] for j in range(1, 7)) + gd[i, 0]
        start(copies_e(i))

    def collect(i):
        other = pl.ds((1 - c) * HALF, HALF)
        remote(fin.at[i, other], fin.at[i, other], ges.at[i], ger.at[i], sibling).wait_recv()
        packed = fin[i]
        turned = pltpu.roll(packed, 64, 1)
        return jnp.concatenate(
            [jnp.where(left[:32], packed, turned), jnp.where(left[:32], turned, packed)], axis=0
        )

    input_1 = (v0[...].astype(F32) * root).astype(BF16)
    xs1[0] = input_1
    sent_1 = exchange(xs1, x1s, x1r)
    start(sent_1)
    arrive(sent_1)
    scaled_1 = (apply_graph(xs1) + degree * input_1.astype(F32)) * root

    wide_2 = scaled_1 * root
    xs2[0] = wide_2.astype(BF16)
    sent_2 = exchange(xs2, x2s, x2r)
    start(sent_2)
    gram(0, scaled_1)
    step_b(0)
    step_c(0)
    step_d(0)
    arrive(sent_2)
    scaled_2 = (apply_graph(xs2) + degree * wide_2) * root
    gram(1, scaled_2)
    step_b(1)
    step_e(0)
    step_c(1)
    gram_1 = collect(0)
    augmented = jnp.where(left, gram_1, jnp.where(lane == row + VEC, 1.0, 0.0))
    blocks = [augmented[8 * i : 8 * i + 8] for i in range(8)]
    blocks = eliminate(blocks, 0, 32)
    step_d(1)
    blocks = eliminate(blocks, 32, VEC)
    inverse_1 = jnp.where(left, 0.0, finish(blocks))
    step_e(1)
    gram_2 = jnp.where(left, 0.0, collect(1))
    half_way = dot32(inverse_1, jnp.concatenate([zeros, gram_2], axis=0))
    middle = dot32(half_way, jnp.concatenate([inverse_1, zeros], axis=0), NT)
    augmented = jnp.where(left, middle, inverse_1)
    blocks = eliminate([augmented[8 * i : 8 * i + 8] for i in range(8)], 0, VEC)
    inverse_2 = jnp.where(left, 0.0, finish(blocks))
    out[...] = dot32(inverse_2, jnp.concatenate([jnp.zeros((VEC, TILE), F32), scaled_2], axis=0))

    for copy in note_out + sent_1 + sent_2 + own_down[:3] + own_facing + on_down:
        copy.wait_send()

    @pl.when(even)
    def _():
        own_down[3].wait_send()

    @pl.when(c == 0)
    def _():
        far_tile.wait_send()

    @pl.when(c == 1)
    def _():
        for copy in near_tiles:
            copy.wait_send()

    for k in (1, 2, 3):
        for p in range(2):
            by_core(hand_on(k, p), left_here)
    for i in range(2):
        for copies in (copies_b, copies_c, copies_d, copies_e):
            for copy in copies(i):
                copy.wait_send()


def shards(tile_values, tile_offset, tile_exponent, initial_vectors):
    dma = pltpu.SemaphoreType.DMA
    tiles = [pltpu.VMEM((ROWS[d], TILE, TILE), BF16) for d in range(1, REACH)]
    basis_t = pl.pallas_call(
        kernel,
        out_shape=jax.ShapeDtypeStruct((VEC, TILE), F32),
        in_specs=[
            pl.BlockSpec(memory_space=pltpu.HBM),
            pl.BlockSpec(memory_space=pltpu.HBM),
            pl.BlockSpec(memory_space=pltpu.HBM),
            pl.BlockSpec(memory_space=pltpu.VMEM),
        ],
        out_specs=pl.BlockSpec(memory_space=pltpu.VMEM),
        scratch_shapes=[
            pltpu.VMEM((SLOTS, TILE, TILE), BF16),
            *tiles,
            pltpu.SMEM((1, SLOTS), jnp.int32),
            pltpu.SMEM((1, SLOTS), jnp.int32),
            pltpu.VMEM((REACH, 8, 128), jnp.int32),
            pltpu.SMEM((REACH, 8, 128), jnp.int32),
            pltpu.VMEM((SLOTS, TILE, TILE), F32),
            pltpu.VMEM((SLOTS, TILE, TILE), BF16),
            pltpu.VMEM((REACH, VEC, TILE), BF16),
            pltpu.VMEM((REACH, VEC, TILE), BF16),
            pltpu.VMEM((2, 2 * HALF, 128), F32),
            pltpu.VMEM((2, 2 * NX - 1, HALF, 128), F32),
            pltpu.VMEM((2, HALF, 128), F32),
            pltpu.VMEM((2, NY - 1, HALF, 128), F32),
            pltpu.VMEM((2, HALF, 128), F32),
            pltpu.VMEM((2, NZ - 1, HALF, 128), F32),
            pltpu.VMEM((2, 2 * HALF, 128), F32),
            dma, dma((2,)), dma,
            dma((20,)), dma((8, 4)),
            dma((8,)), dma((8,)),
            dma((8,)), dma((8,)),
            dma((8,)), dma((8,)),
            dma((2, 2 * NX - 1)), dma((2, 2 * NX - 1)),
            dma((2, NY - 1)), dma((2, NY - 1)),
            dma((2, NZ - 1)), dma((2, NZ - 1)),
            dma((2,)), dma((2,)),
        ],
        compiler_params=pltpu.CompilerParams(
            collective_id=0, has_side_effects=True, vmem_limit_bytes=40 * 1024 * 1024
        ),
        cost_estimate=pl.CostEstimate(flops=1200000000, bytes_accessed=1000000, transcendentals=0),
        name="embed",
    )(tile_values, tile_offset, tile_exponent, initial_vectors.T)
    return basis_t.T


def solution(mesh):
    return jax.shard_map(
        shards,
        mesh=mesh,
        in_specs=(
            P(("grp", "blk"), None, None, None),
            P(("grp", "blk"), None),
            P(("grp", "blk"), None),
            P(("grp", "blk"), None),
        ),
        out_specs=P(("grp", "blk"), None),
        check_vma=False,
    )
```

time: 121 us -> 93.9 us (0.78)
  Pallas kernels: 118 us -> 90.4 us
    pallas_call x1, Pallas kernels: 118 us -> 90.4 us  [shards(): pl.pallas_call(kernel, out_shape=jax.ShapeDtypeStruct((VEC, TILE), F32),...]
    unnamed x8 -> x9, local copies, waits for them, and re-layouts: 2.66 us -> 3.19 us
where the time goes in v2:
time: 93.9 us; the launch traced here: 93.6 us
  Pallas kernels  90.4 us (96%)
  local copies, waits for them, and re-layouts  3.19 us (3%)
    pallas_call x1, Pallas kernels, shards(): pl.pallas_call(kernel, out_shape=jax.ShapeDtypeStruct((VEC, TILE), F32),...  90.4 us
    unnamed x9, local copies, waits for them, and re-layouts  3.19 us

profile of v2, /device:TPU:1, one launch (start us, length us, event | category | flops | bytes accessed | tf_op | source)
XLA Modules:
  0.0 93.6 jit_solution(16747110966026001413)
XLA Ops:
  0.0 0.0 copy-start.3
  0.0 0.0 copy-start.2
  0.0 0.7 copy-done.3
  0.7 0.0 copy-done.2
  0.7 0.0 copy-start
  0.7 1.1 %copy-done = bf16[1,6,256,256]{3,2,1,0:T(8,128)(2,1)S(1)} copy-done((bf16[1,6,256,256]{3,2,1,0:T(8,128)(2,1)S(1)}, bf16[1,6,256,256]{3,2,1,0:T(8,128)(2,1)}, u32[]{:S(2)}) %copy-start) | copy-done | bytes 786456
  1.8 0.0 copy-start.1
  1.8 0.8 copy-done.1
  2.6 90.4 %embed.1 = f32[64,256]{1,0:T(8,128)S(1)} custom-call(bf16[1,6,256,256]{3,2,1,0:T(8,128)(2,1)S(1)} %copy-done, s32[1,6]{1,0:T(1,128)S(1)} %copy-done.2, s32[1,6]{1,0:T(1,128)S(1)} %copy-done.3, bf16[64,256]{1,0:T(8,128)(2,1)S(1)} %bitcast.3), custom_call_target="tpu_custom_call" | custom-call | flops 1200000000 | bytes 1000000 | tf_op jit(solution)/shard_map/embed/pallas_call | solution.py:439
  93.0 0.6 copy.6
Async XLA Ops:
  0.0 0.7 copy-start.3
  0.0 0.7 copy-start.2
  0.7 1.1 %copy-start = (bf16[1,6,256,256]{3,2,1,0:T(8,128)(2,1)S(1)}, bf16[1,6,256,256]{3,2,1,0:T(8,128)(2,1)}, u32[]{:S(2)}) copy-start(bf16[1,6,256,256]{3,2,1,0:T(8,128)(2,1)} %tv.1) | copy-start | bytes 2359300
  1.8 0.8 copy-start.1

commit v3 on v2

--- a/solution.py
+++ b/solution.py
@@ -17,7 +17,9 @@
 F32 = jnp.float32
 BF16 = jnp.bfloat16
 NEED = [min(SLOTS, REACH - d) for d in range(REACH)]
-PIECES = [(0, 1), (1, 3), (3, 5), (5, 6)]
+SECOND = [5, 4]
+THIRD = [3, 2]
+ACROSS = (1, 2)
 PARTS = {1: [(0, 3), (3, 6)], 3: [(0, 3), (3, 5)], 5: [(0, 3)], 7: [(0, 1)]}
 ROWS = {1: 6, 2: 6, 3: 5, 4: 6, 5: 3, 6: 3, 7: 1}
 NT = (((1,), (1,)), ((), ()))
@@ -93,9 +95,9 @@
 
 def kernel(
     tv, off_any, ex_any, v0, out,
-    own, rb1, rb2, rb3, rb4, rb5, rb6, rb7, off, ex, meta, smeta, paths, motif, xs1, xs2,
+    own, rb1, rb2, rb3, rb4, rb5, rb6, rb7, off, ex, meta, smeta, paths, motif, vs, roots, xs2,
     g_src, gb, gc_src, gc, gd_src, gd, fin,
-    own_sem, in_sem, smeta_sem, ts, tr, ms, mr, x1s, x1r, x2s, x2r,
+    own_sem, in_sem, smeta_sem, ts, tr, tp, ms, mr, vsend, vrecv, rsend, rrecv, x2s, x2r,
     gbs, gbr, gcs, gcr, gds, gdr, ges, ger,
 ):
     rb = {1: rb1, 2: rb2, 3: rb3, 4: rb4, 5: rb5, 6: rb6, 7: rb7}
@@ -122,6 +124,7 @@
     sibling = at_blk(q, 1 - c)
     cross = at_blk(q - 4 + 8 * c, 1 - c)
     facing = at_blk(q + 1 - 2 * x_hi, c)
+    even, odd = x_hi == 0, x_hi == 1
     below = at_blk(q - 2, c)
     x_mates = [at_xyz(lax.rem(x + j, NX), y, z) for j in range(1, NX)]
     x_others = [at_xyz(lax.rem(x + j, NX), y, z, 1 - c) for j in range(NX)]
@@ -140,9 +143,11 @@
     load_ex = pltpu.make_async_copy(ex_any, ex, in_sem.at[1])
     load_off.start()
     load_ex.start()
+    load_v0 = pltpu.make_async_copy(v0, vs.at[0], in_sem.at[2])
+    load_v0.start()
 
     barrier = pltpu.get_barrier_semaphore()
-    met = x_mates + x_others[1:] + y_mates + z_mates
+    met = [x_mates[0], x_mates[2], x_others[1], x_others[3]] + y_mates + z_mates[1:-1]
     for d in range(1, REACH):
         met.append(at_behind(d))
         met.append(at_behind(-d))
@@ -160,55 +165,51 @@
     meta[0] = note
     pl.semaphore_wait(barrier, len(met))
 
-    def piece(src, d, j, sem, dev):
-        lo, hi = PIECES[j]
-        return remote(src.at[pl.ds(lo, hi - lo)], rb[d].at[pl.ds(lo, hi - lo)], ts.at[sem + j], tr.at[d, j], dev)
+    def one_tile(src, d, j, sem, dev):
+        return remote(src.at[j], rb[d].at[j], ts.at[sem + j], tr.at[d, j], dev)
 
     mine = tv.at[0]
-    own_down = [piece(mine, 4, j, 0, below) for j in range(4)]
-    own_facing = [piece(mine, 2, j, 4, facing) for j in range(4)]
-    on_facing = [piece(rb4, 2, j, 4, facing) for j in range(4)]
-    on_down = [piece(rb2, 6, j, 8, below) for j in range(2)]
-    far_tile = remote(tv.at[0, pl.ds(0, 1)], rb7, ts.at[10], tr.at[7, 0], cross)
+    own_down = [one_tile(mine, 4, j, 0, below) for j in range(6)]
+    own_facing = [one_tile(mine, 2, j, 6, facing) for j in range(6)]
+    on_facing = [one_tile(rb4, 2, j, 6, facing) for j in range(6)]
+    on_down = [one_tile(rb2, 6, j, 12, below) for j in range(3)]
+    across = [one_tile(rb4, 6, j, 15, facing) for j in range(3)]
+    far_tile = remote(rb4.at[0], rb7.at[0], ts.at[18], tp.at[7, 0], at_blk(q - 2, 1))
+
+    def both(*tests):
+        keep = tests[0]
+        for test in tests[1:]:
+            keep = jnp.logical_and(keep, test)
+        return keep
+
+    def up_to(j, limits):
+        return c >= 0 if j < limits[1] else (c == 0 if j < limits[0] else c < 0)
+
+    def comes_down(j):
+        return jnp.logical_or(even, up_to(j, SECOND))
 
     def part(src, d, p, sem):
         lo, hi = PARTS[d][p]
-        return remote(src.at[pl.ds(lo, hi - lo)], rb[d].at[pl.ds(lo, hi - lo)], ts.at[sem + p], tr.at[d, p], sibling)
-
-    near_tiles = [part(mine, 1, p, 11) for p in range(2)]
+        return remote(src.at[pl.ds(lo, hi - lo)], rb[d].at[pl.ds(lo, hi - lo)], ts.at[sem + p], tp.at[d, p], sibling)
+
+    def vectors(src, d, sem, dev):
+        return remote(vs.at[src], vs.at[d], vsend.at[sem], vrecv.at[d], dev)
+
+    v_down = vectors(0, 4, 0, below)
+    v_facing = vectors(0, 2, 1, facing)
+    v_on_facing = vectors(4, 2, 1, facing)
+    v_on_down = vectors(2, 6, 2, below)
+    v_across = vectors(4, 6, 3, facing)
+    v_far = vectors(4, 7, 4, at_blk(q - 2, 1))
+    v_near = vectors(0, 1, 5, sibling)
+    v_hand_on = [None] + [[vectors(2 * k, d, 5 + k, sibling) for d in (2 * k - 1, 2 * k + 1)] for k in (1, 2, 3)]
+
+    near_tiles = [part(mine, 1, p, 19) for p in range(2)]
     note_out = [
         remote(meta.at[0], meta.at[d], ms.at[d], mr.at[d], at_behind(d)) for d in range(1, REACH)
     ]
-    even, odd = x_hi == 0, x_hi == 1
     for copy in note_out:
         copy.start()
-
-    @pl.when(even)
-    def _():
-        for j in range(4):
-            own_down[j].start()
-
-    @pl.when(odd)
-    def _():
-        for j in range(4):
-            own_facing[j].start()
-            if j < 3:
-                own_down[j].start()
-
-    @pl.when(c == 1)
-    def _():
-        for copy in near_tiles:
-            copy.start()
-
-    @pl.when(c == 0)
-    def _():
-        far_tile.start()
-
-    def hand_on(k, p):
-        return [
-            part(rb[2 * k], d, p, 11 + 2 * k) if p < len(PARTS[d]) else None
-            for d in (2 * k - 1, 2 * k + 1)
-        ]
 
     def by_core(copies, act):
         for core in range(2):
@@ -223,9 +224,36 @@
     def left_here(copy):
         copy.wait_send()
 
+    def has_come(copy):
+        copy.wait_recv()
+
+    def when(test, act, copy):
+        @pl.when(test)
+        def _():
+            act(copy)
+
+    for j in range(6):
+        when(odd, go, own_facing[j])
+        when(comes_down(j), go, own_down[j])
+    load_v0.wait()
+    when(odd, go, v_facing)
+    v_down.start()
+    when(c == 1, go, v_near)
+
+    @pl.when(c == 1)
+    def _():
+        for copy in near_tiles:
+            copy.start()
+
+    def hand_on(k, p):
+        return [
+            part(rb[2 * k], d, p, 19 + 2 * k) if p < len(PARTS[d]) else None
+            for d in (2 * k - 1, 2 * k + 1)
+        ]
+
     def here(d):
         for p in range(len(PARTS[d])):
-            part(rb[d], d, p, 11).wait_recv()
+            part(rb[d], d, p, 19).wait_recv()
 
     def absorb(d, right_ref, first):
         slot = jnp.int32(0)
@@ -253,20 +281,17 @@
 
         lax.fori_loop(0 if d == 0 else max(1, d - 2), SLOTS, one, 0)
 
-    for j in range(4):
+    for j in range(6):
+        when(comes_down(j), has_come, own_down[j])
+        if j == 0:
+            when(c == 0, go, far_tile)
+        when(even, go, on_facing[j])
+        if j in ACROSS:
+            when(both(odd, up_to(j, THIRD)), go, across[j])
+        own_facing[j].wait_recv()
         if j < 3:
-            own_down[j].wait_recv()
-
-        @pl.when(even)
-        def _(j=j):
-            if j == 3:
-                own_down[j].wait_recv()
-            on_facing[j].start()
-
-        own_facing[j].wait_recv()
-        if j < 2:
-            on_down[j].start()
-        if j == 1:
+            when(both(odd, up_to(j, THIRD)) if j in ACROSS else up_to(j, THIRD), go, on_down[j])
+        if j == 2:
             by_core(hand_on(1, 0), go)
             by_core(hand_on(2, 0), go)
             for copy in note_out:
@@ -276,18 +301,29 @@
             to_scalar.wait()
             load_own.wait()
             absorb(0, own, True)
-        if j == 2:
+        if j == 4:
             by_core(hand_on(2, 1), go)
     by_core(hand_on(1, 1), go)
+    v_down.wait_recv()
+    when(even, go, v_on_facing)
+    when(odd, go, v_across)
+    when(c == 0, go, v_far)
+    by_core(v_hand_on[2], go)
     absorb(4, rb4, False)
     absorb(2, rb2, False)
-    for j in range(2):
-        on_down[j].wait_recv()
+    for j in range(3):
+        when(up_to(j, THIRD), has_come, on_down[j])
     by_core(hand_on(3, 0), go)
+    v_facing.wait_recv()
+    when(odd, go, v_on_down)
+    by_core(v_hand_on[1], go)
     absorb(6, rb6, False)
     for d in (1, 3, 5, 7):
         here(d)
         absorb(d, rb[d], False)
+
+    v_on_down.wait_recv()
+    by_core(v_hand_on[3], go)
 
     ones = jnp.ones((8, TILE), BF16)
     degree = jnp.zeros((8, TILE), F32)
@@ -299,7 +335,40 @@
     root = lax.rsqrt(degree)
 
     def exchange(xs, ssem, rsem):
-        return [remote(xs.at[0], xs.at[d], ssem.at[d], rsem.at[d], at_behind(d)) for d in range(1, REACH)]
+        direct = [
+            remote(xs.at[0], xs.at[2 * k], ssem.at[k], rsem.at[2 * k], at_blk(q - k, c)) for k in (1, 2, 3)
+        ]
+        far = remote(xs.at[0], xs.at[7], ssem.at[4], rsem.at[7], cross)
+        near = remote(xs.at[0], xs.at[1], ssem.at[5], rsem.at[1], sibling)
+        direct[2].start()
+        by_core([far, near], go)
+        direct[1].start()
+        direct[0].start()
+        return direct
+
+    def passing(xs, ssem, rsem, k):
+        return [
+            remote(xs.at[2 * k], xs.at[d], ssem.at[5 + k], rsem.at[d], sibling)
+            for d in (2 * k - 1, 2 * k + 1)
+        ]
+
+    def relay(xs, ssem, rsem, direct):
+        for k in (1, 2, 3):
+            direct[k - 1].wait_recv()
+            by_core(passing(xs, ssem, rsem, k), go)
+
+    def rest(xs, ssem, rsem):
+        for d in (1, 3, 5, 7):
+            remote(xs.at[d], xs.at[d], ssem.at[0], rsem.at[d], sibling).wait_recv()
+
+    def all_left(xs, ssem, rsem, direct):
+        for copy in direct:
+            copy.wait_send()
+        far = remote(xs.at[0], xs.at[7], ssem.at[4], rsem.at[7], cross)
+        near = remote(xs.at[0], xs.at[1], ssem.at[5], rsem.at[1], sibling)
+        by_core([far, near], left_here)
+        for k in (1, 2, 3):
+            by_core(passing(xs, ssem, rsem, k), left_here)
 
     def apply_graph(xs):
         total = jnp.zeros((VEC, TILE), F32)
@@ -371,33 +440,39 @@
             [jnp.where(left[:32], packed, turned), jnp.where(left[:32], turned, packed)], axis=0
         )
 
-    input_1 = (v0[...].astype(F32) * root).astype(BF16)
-    xs1[0] = input_1
-    sent_1 = exchange(xs1, x1s, x1r)
-    start(sent_1)
-    arrive(sent_1)
-    scaled_1 = (apply_graph(xs1) + degree * input_1.astype(F32)) * root
+    roots[0] = root
+    root_out = [
+        remote(roots.at[0], roots.at[d], rsend.at[d], rrecv.at[d], at_behind(d)) for d in (7, 6, 5, 4, 3, 2, 1)
+    ]
+    start(root_out)
+    for d in (1, 3, 5, 7):
+        vectors(0, d, 0, sibling).wait_recv()
+    arrive(root_out)
+    total = jnp.zeros((VEC, TILE), F32)
+    for s in range(SLOTS):
+        input_s = (vs[offs[s]].astype(F32) * roots[offs[s]]).astype(BF16)
+        total = total + lax.dot_general(input_s, motif[s], NT, preferred_element_type=F32)
+    input_1 = (vs[0].astype(F32) * root).astype(BF16).astype(F32)
+    scaled_1 = (total + degree * input_1) * root
 
     wide_2 = scaled_1 * root
     xs2[0] = wide_2.astype(BF16)
     sent_2 = exchange(xs2, x2s, x2r)
-    start(sent_2)
     gram(0, scaled_1)
     step_b(0)
+    relay(xs2, x2s, x2r, sent_2)
     step_c(0)
-    step_d(0)
-    arrive(sent_2)
+    rest(xs2, x2s, x2r)
     scaled_2 = (apply_graph(xs2) + degree * wide_2) * root
     gram(1, scaled_2)
     step_b(1)
+    step_d(0)
+    step_c(1)
     step_e(0)
-    step_c(1)
+    step_d(1)
     gram_1 = collect(0)
     augmented = jnp.where(left, gram_1, jnp.where(lane == row + VEC, 1.0, 0.0))
-    blocks = [augmented[8 * i : 8 * i + 8] for i in range(8)]
-    blocks = eliminate(blocks, 0, 32)
-    step_d(1)
-    blocks = eliminate(blocks, 32, VEC)
+    blocks = eliminate([augmented[8 * i : 8 * i + 8] for i in range(8)], 0, VEC)
     inverse_1 = jnp.where(left, 0.0, finish(blocks))
     step_e(1)
     gram_2 = jnp.where(left, 0.0, collect(1))
@@ -408,12 +483,15 @@
     inverse_2 = jnp.where(left, 0.0, finish(blocks))
     out[...] = dot32(inverse_2, jnp.concatenate([jnp.zeros((VEC, TILE), F32), scaled_2], axis=0))
 
-    for copy in note_out + sent_1 + sent_2 + own_down[:3] + own_facing + on_down:
+    for copy in note_out:
         copy.wait_send()
-
-    @pl.when(even)
-    def _():
-        own_down[3].wait_send()
+    for j in range(6):
+        when(comes_down(j), left_here, own_down[j])
+        own_facing[j].wait_send()
+        if j < 3:
+            when(both(odd, up_to(j, THIRD)) if j in ACROSS else up_to(j, THIRD), left_here, on_down[j])
+        if j in ACROSS:
+            when(both(odd, up_to(j, THIRD)), left_here, across[j])
 
     @pl.when(c == 0)
     def _():
@@ -424,6 +502,16 @@
         for copy in near_tiles:
             copy.wait_send()
 
+    for copy in [v_down] + root_out:
+        copy.wait_send()
+    v_facing.wait_send()
+    when(odd, left_here, v_across)
+    when(odd, left_here, v_on_down)
+    when(c == 0, left_here, v_far)
+    when(c == 1, left_here, v_near)
+    for k in (1, 2, 3):
+        by_core(v_hand_on[k], left_here)
+    all_left(xs2, x2s, x2r, sent_2)
     for k in (1, 2, 3):
         for p in range(2):
             by_core(hand_on(k, p), left_here)
@@ -443,7 +531,7 @@
             pl.BlockSpec(memory_space=pltpu.HBM),
             pl.BlockSpec(memory_space=pltpu.HBM),
             pl.BlockSpec(memory_space=pltpu.HBM),
-            pl.BlockSpec(memory_space=pltpu.VMEM),
+            pl.BlockSpec(memory_space=pltpu.HBM),
         ],
         out_specs=pl.BlockSpec(memory_space=pltpu.VMEM),
         scratch_shapes=[
@@ -456,6 +544,7 @@
             pltpu.VMEM((SLOTS, TILE, TILE), F32),
             pltpu.VMEM((SLOTS, TILE, TILE), BF16),
             pltpu.VMEM((REACH, VEC, TILE), BF16),
+            pltpu.VMEM((REACH, 1, TILE), F32),
             pltpu.VMEM((REACH, VEC, TILE), BF16),
             pltpu.VMEM((2, 2 * HALF, 128), F32),
             pltpu.VMEM((2, 2 * NX - 1, HALF, 128), F32),
@@ -464,18 +553,19 @@
             pltpu.VMEM((2, HALF, 128), F32),
             pltpu.VMEM((2, NZ - 1, HALF, 128), F32),
             pltpu.VMEM((2, 2 * HALF, 128), F32),
-            dma, dma((2,)), dma,
-            dma((20,)), dma((8, 4)),
+            dma, dma((3,)), dma,
+            dma((27,)), dma((8, 6)), dma((8, 2)),
             dma((8,)), dma((8,)),
+            dma((9,)), dma((8,)),
             dma((8,)), dma((8,)),
-            dma((8,)), dma((8,)),
+            dma((9,)), dma((8,)),
             dma((2, 2 * NX - 1)), dma((2, 2 * NX - 1)),
             dma((2, NY - 1)), dma((2, NY - 1)),
             dma((2, NZ - 1)), dma((2, NZ - 1)),
             dma((2,)), dma((2,)),
         ],
         compiler_params=pltpu.CompilerParams(
-            collective_id=0, has_side_effects=True, vmem_limit_bytes=40 * 1024 * 1024
+            collective_id=0, has_side_effects=True, vmem_limit_bytes=55000 * 1024
         ),
         cost_estimate=pl.CostEstimate(flops=1200000000, bytes_accessed=1000000, transcendentals=0),
         name="embed",

time: 93.9 us -> 83.3 us (0.89)
  Pallas kernels: 90.4 us -> 81.1 us
  local copies, waits for them, and re-layouts: 3.19 us -> 2.06 us
    pallas_call x1, Pallas kernels: 90.4 us -> 81.1 us  [shards(): pl.pallas_call(kernel, out_shape=jax.ShapeDtypeStruct((VEC, TILE), F32),...]
    unnamed x9 -> x7, local copies, waits for them, and re-layouts: 3.19 us -> 2.06 us
where the time goes in v3:
time: 83.3 us; the launch traced here: 83.1 us
  Pallas kernels  81.1 us (97%)
  local copies, waits for them, and re-layouts  2.06 us (2%)
    pallas_call x1, Pallas kernels, shards(): pl.pallas_call(kernel, out_shape=jax.ShapeDtypeStruct((VEC, TILE), F32),...  81.1 us
    unnamed x7, local copies, waits for them, and re-layouts  2.06 us

profile of v3, /device:TPU:1, one launch (start us, length us, event | category | flops | bytes accessed | tf_op | source)
XLA Modules:
  0.0 83.1 jit_solution(6656786145050571153)
XLA Ops:
  0.0 0.0 copy-start.2
  0.0 0.0 copy-start.1
  0.0 0.7 copy-done.2
  0.7 0.0 copy-done.1
  0.7 0.0 copy-start
  0.7 0.8 copy-done
  1.4 81.1 %embed.1 = f32[64,256]{1,0:T(8,128)S(1)} custom-call(bf16[1,6,256,256]{3,2,1,0:T(8,128)(2,1)} %tv.1, s32[1,6]{1,0:T(1,128)S(1)} %copy-done.1, s32[1,6]{1,0:T(1,128)S(1)} %copy-done.2, bf16[64,256]{1,0:T(8,128)(2,1)S(1)} %bitcast.3), custom_call_target="tpu_custom_call" | custom-call | flops 1200000000 | bytes 1000000 | tf_op jit(solution)/shard_map/embed/pallas_call | solution.py:527
  82.5 0.6 copy.6
Async XLA Ops:
  0.0 0.7 copy-start.2
  0.0 0.7 copy-start.1
  0.7 0.8 copy-start

commit v4 on v3

--- a/solution.py
+++ b/solution.py
@@ -13,6 +13,7 @@
 BLK = 32
 CHIPS = 16
 NX, NY, NZ = 4, 8, 8
+RING = (4, 3, 5, 2, 6, 1, 7)
 HALF = 16
 F32 = jnp.float32
 BF16 = jnp.bfloat16
@@ -20,7 +21,7 @@
 SECOND = [5, 4]
 THIRD = [3, 2]
 ACROSS = (1, 2)
-PARTS = {1: [(0, 3), (3, 6)], 3: [(0, 3), (3, 5)], 5: [(0, 3)], 7: [(0, 1)]}
+PARTS = {1: [(0, 3), (3, 5), (5, 6)], 3: [(0, 3), (3, 5)], 5: [(0, 3)], 7: [(0, 1)]}
 ROWS = {1: 6, 2: 6, 3: 5, 4: 6, 5: 3, 6: 3, 7: 1}
 NT = (((1,), (1,)), ((), ()))
 
@@ -37,6 +38,12 @@
     return lax.dot_general(
         a, b, dims, precision=lax.Precision.HIGHEST, preferred_element_type=F32
     )
+
+
+def reciprocal(x):
+    guess = pl.reciprocal(x, approx=True)
+    guess = guess * (2.0 - x * guess)
+    return guess * (2.0 - x * guess)
 
 
 def eliminate(blocks, first, last):
@@ -56,13 +63,20 @@
         upper = [spread(head[kr + j : kr + j + 1, :]) for j in range(4)]
         corner = [[spread(columns[kb][j][kr + a : kr + a + 1, :]) for j in range(4)] for a in range(4)]
         inverse = []
-        for a in range(4):
-            inverse.append(1.0 / corner[a][a])
-            for r in range(a + 1, 4):
-                low = corner[a][r] * inverse[a]
-                for j in range(r, 4):
-                    corner[r][j] = corner[r][j] - low * corner[a][j]
-                upper[r] = upper[r] - low * upper[a]
+        for a in (0, 2):
+            inverse.append(reciprocal(corner[a][a]))
+            low = corner[a][a + 1] * inverse[a]
+            minor = corner[a][a] * corner[a + 1][a + 1] - corner[a][a + 1] * corner[a][a + 1]
+            inverse.append(corner[a][a] * reciprocal(minor))
+            for j in range(a + 1, 4):
+                corner[a + 1][j] = corner[a + 1][j] - low * corner[a][j]
+            upper[a + 1] = upper[a + 1] - low * upper[a]
+            for r in range(a + 2, 4):
+                for e in (a, a + 1):
+                    low = corner[e][r] * inverse[e]
+                    for j in range(r, 4):
+                        corner[r][j] = corner[r][j] - low * corner[e][j]
+                    upper[r] = upper[r] - low * upper[e]
         for i in range(kb, 8):
             if i == kb and kr == 4:
                 continue
@@ -126,10 +140,10 @@
     facing = at_blk(q + 1 - 2 * x_hi, c)
     even, odd = x_hi == 0, x_hi == 1
     below = at_blk(q - 2, c)
-    x_mates = [at_xyz(lax.rem(x + j, NX), y, z) for j in range(1, NX)]
-    x_others = [at_xyz(lax.rem(x + j, NX), y, z, 1 - c) for j in range(NX)]
-    y_mates = [at_xyz(x, lax.rem(y + j, NY), z) for j in range(1, NY)]
-    z_mates = [at_xyz(x, y, lax.rem(z + j, NZ)) for j in range(1, NZ)]
+    x_mates = [at_xyz(lax.rem(x + j, NX), y, z) for j in (2, 1, 3)]
+    x_others = [at_xyz(lax.rem(x + j, NX), y, z, 1 - c) for j in (2, 1, 3, 0)]
+    y_mates = [at_xyz(x, lax.rem(y + j, NY), z) for j in RING]
+    z_mates = [at_xyz(x, y, lax.rem(z + j, NZ)) for j in RING]
 
     def remote(src, dst, ssem, rsem, dev):
         return pltpu.make_async_remote_copy(
@@ -147,8 +161,8 @@
     load_v0.start()
 
     barrier = pltpu.get_barrier_semaphore()
-    met = [x_mates[0], x_mates[2], x_others[1], x_others[3]] + y_mates + z_mates[1:-1]
-    for d in range(1, REACH):
+    met = y_mates + z_mates[:5] + x_mates[1:] + x_others[1:3]
+    for d in range(REACH - 1, 0, -1):
         met.append(at_behind(d))
         met.append(at_behind(-d))
     for dev in met:
@@ -204,13 +218,10 @@
     v_near = vectors(0, 1, 5, sibling)
     v_hand_on = [None] + [[vectors(2 * k, d, 5 + k, sibling) for d in (2 * k - 1, 2 * k + 1)] for k in (1, 2, 3)]
 
-    near_tiles = [part(mine, 1, p, 19) for p in range(2)]
+    near_tiles = [part(mine, 1, p, 19) for p in range(3)]
     note_out = [
-        remote(meta.at[0], meta.at[d], ms.at[d], mr.at[d], at_behind(d)) for d in range(1, REACH)
+        remote(meta.at[0], meta.at[d], ms.at[d], mr.at[d], at_behind(d)) for d in range(REACH - 1, 0, -1)
     ]
-    for copy in note_out:
-        copy.start()
-
     def by_core(copies, act):
         for core in range(2):
             if copies[core] is not None:
@@ -232,7 +243,9 @@
         def _():
             act(copy)
 
-    for j in range(6):
+    for copy in note_out:
+        copy.start()
+    for j in range(SLOTS):
         when(odd, go, own_facing[j])
         when(comes_down(j), go, own_down[j])
     load_v0.wait()
@@ -247,7 +260,7 @@
 
     def hand_on(k, p):
         return [
-            part(rb[2 * k], d, p, 19 + 2 * k) if p < len(PARTS[d]) else None
+            part(rb[2 * k], d, p, 19 + 3 * k) if p < len(PARTS[d]) else None
             for d in (2 * k - 1, 2 * k + 1)
         ]
 
@@ -279,7 +292,7 @@
                 paths[s] = paths[s] + product
             return carry
 
-        lax.fori_loop(0 if d == 0 else max(1, d - 2), SLOTS, one, 0)
+        lax.fori_loop(0 if d == 0 else max(1, d - 2), SLOTS, one, 0, unroll=True)
 
     for j in range(6):
         when(comes_down(j), has_come, own_down[j])
@@ -302,8 +315,9 @@
             load_own.wait()
             absorb(0, own, True)
         if j == 4:
+            by_core(hand_on(1, 1), go)
             by_core(hand_on(2, 1), go)
-    by_core(hand_on(1, 1), go)
+    by_core(hand_on(1, 2), go)
     v_down.wait_recv()
     when(even, go, v_on_facing)
     when(odd, go, v_across)
@@ -387,13 +401,13 @@
 
     def copies_b(i):
         own_half, other_half = pl.ds(c * HALF, HALF), pl.ds((1 - c) * HALF, HALF)
-        return [
-            remote(g_src.at[i, other_half], gb.at[i, 3 + j], gbs.at[i, 3 + j], gbr.at[i, 3 + j], x_others[j])
-            for j in range(NX)
-        ] + [
-            remote(g_src.at[i, own_half], gb.at[i, j], gbs.at[i, j], gbr.at[i, j], x_mates[j])
-            for j in range(NX - 1)
-        ]
+        copies = []
+        for j in range(NX):
+            copies.append(remote(g_src.at[i, other_half], gb.at[i, j], gbs.at[i, j], gbr.at[i, j], x_others[j]))
+            if j < NX - 1:
+                n = NX + j
+                copies.append(remote(g_src.at[i, own_half], gb.at[i, n], gbs.at[i, n], gbr.at[i, n], x_mates[j]))
+        return copies
 
     def copies_c(i):
         return [remote(gc_src.at[i], gc.at[i, j], gcs.at[i, j], gcr.at[i, j], y_mates[j]) for j in range(NY - 1)]
@@ -513,7 +527,7 @@
         by_core(v_hand_on[k], left_here)
     all_left(xs2, x2s, x2r, sent_2)
     for k in (1, 2, 3):
-        for p in range(2):
+        for p in range(3):
             by_core(hand_on(k, p), left_here)
     for i in range(2):
         for copies in (copies_b, copies_c, copies_d, copies_e):
@@ -554,7 +568,7 @@
             pltpu.VMEM((2, NZ - 1, HALF, 128), F32),
             pltpu.VMEM((2, 2 * HALF, 128), F32),
             dma, dma((3,)), dma,
-            dma((27,)), dma((8, 6)), dma((8, 2)),
+            dma((31,)), dma((8, 6)), dma((8, 3)),
             dma((8,)), dma((8,)),
             dma((9,)), dma((8,)),
             dma((8,)), dma((8,)),

time: 83.3 us -> 81.1 us (0.974)
  Pallas kernels: 81.1 us -> 78.8 us
    pallas_call x1, Pallas kernels: 81.1 us -> 78.8 us  [shards(): pl.pallas_call(kernel, out_shape=jax.ShapeDtypeStruct((VEC, TILE), F32),...]
where the time goes in v4:
time: 81.1 us; the launch traced here: 80.9 us
  Pallas kernels  78.8 us (97%)
  local copies, waits for them, and re-layouts  2.06 us (3%)
    pallas_call x1, Pallas kernels, shards(): pl.pallas_call(kernel, out_shape=jax.ShapeDtypeStruct((VEC, TILE), F32),...  78.8 us
    unnamed x7, local copies, waits for them, and re-layouts  2.06 us

profile of v4, /device:TPU:1, one launch (start us, length us, event | category | flops | bytes accessed | tf_op | source)
XLA Modules:
  0.0 80.9 jit_solution(10411778374161001042)
XLA Ops:
  0.0 0.0 copy-start.2
  0.0 0.0 copy-start.1
  0.0 0.7 copy-done.2
  0.7 0.0 copy-done.1
  0.7 0.0 copy-start
  0.7 0.8 copy-done
  1.4 78.8 %embed.1 = f32[64,256]{1,0:T(8,128)S(1)} custom-call(bf16[1,6,256,256]{3,2,1,0:T(8,128)(2,1)} %tv.1, s32[1,6]{1,0:T(1,128)S(1)} %copy-done.1, s32[1,6]{1,0:T(1,128)S(1)} %copy-done.2, bf16[64,256]{1,0:T(8,128)(2,1)S(1)} %bitcast.3), custom_call_target="tpu_custom_call" | custom-call | flops 1200000000 | bytes 1000000 | tf_op jit(solution)/shard_map/embed/pallas_call | solution.py:541
  80.3 0.6 copy.6
Async XLA Ops:
  0.0 0.7 copy-start.2
  0.0 0.7 copy-start.1
  0.7 0.8 copy-start

commit v5 on v4

--- a/solution.py
+++ b/solution.py
@@ -210,11 +210,9 @@
         return remote(vs.at[src], vs.at[d], vsend.at[sem], vrecv.at[d], dev)
 
     v_down = vectors(0, 4, 0, below)
-    v_facing = vectors(0, 2, 1, facing)
-    v_on_facing = vectors(4, 2, 1, facing)
-    v_on_down = vectors(2, 6, 2, below)
-    v_across = vectors(4, 6, 3, facing)
-    v_far = vectors(4, 7, 4, at_blk(q - 2, 1))
+    v_facing = vectors(0, 2, 1, at_blk(q - 1, c))
+    v_on_down = vectors(0, 6, 2, at_blk(q - 3, c))
+    v_far = vectors(0, 7, 4, cross)
     v_near = vectors(0, 1, 5, sibling)
     v_hand_on = [None] + [[vectors(2 * k, d, 5 + k, sibling) for d in (2 * k - 1, 2 * k + 1)] for k in (1, 2, 3)]
 
@@ -249,8 +247,6 @@
         when(odd, go, own_facing[j])
         when(comes_down(j), go, own_down[j])
     load_v0.wait()
-    when(odd, go, v_facing)
-    v_down.start()
     when(c == 1, go, v_near)
 
     @pl.when(c == 1)
@@ -314,30 +310,25 @@
             to_scalar.wait()
             load_own.wait()
             absorb(0, own, True)
+        if j == 3:
+            v_on_down.start()
+            when(c == 0, go, v_far)
+            v_facing.start()
+            v_down.start()
         if j == 4:
             by_core(hand_on(1, 1), go)
             by_core(hand_on(2, 1), go)
     by_core(hand_on(1, 2), go)
-    v_down.wait_recv()
-    when(even, go, v_on_facing)
-    when(odd, go, v_across)
-    when(c == 0, go, v_far)
-    by_core(v_hand_on[2], go)
     absorb(4, rb4, False)
     absorb(2, rb2, False)
     for j in range(3):
         when(up_to(j, THIRD), has_come, on_down[j])
     by_core(hand_on(3, 0), go)
-    v_facing.wait_recv()
-    when(odd, go, v_on_down)
-    by_core(v_hand_on[1], go)
     absorb(6, rb6, False)
     for d in (1, 3, 5, 7):
         here(d)
         absorb(d, rb[d], False)
 
-    v_on_down.wait_recv()
-    by_core(v_hand_on[3], go)
 
     ones = jnp.ones((8, TILE), BF16)
     degree = jnp.zeros((8, TILE), F32)
@@ -454,11 +445,50 @@
             [jnp.where(left[:32], packed, turned), jnp.where(left[:32], turned, packed)], axis=0
         )
 
+    def left_all(copies):
+        for copy in copies:
+            copy.wait_send()
+
+    def tiles_have_left():
+        left_all(note_out + [v_down, v_facing, v_on_down])
+        for j in range(SLOTS):
+            when(comes_down(j), left_here, own_down[j])
+            own_facing[j].wait_send()
+            if j < 3:
+                when(both(odd, up_to(j, THIRD)) if j in ACROSS else up_to(j, THIRD), left_here, on_down[j])
+            if j in ACROSS:
+                when(both(odd, up_to(j, THIRD)), left_here, across[j])
+
+        @pl.when(c == 0)
+        def _():
+            left_all([far_tile, v_far])
+
+        @pl.when(c == 1)
+        def _():
+            left_all(near_tiles + [v_near])
+
+        for core in range(2):
+            @pl.when(c == core)
+            def _(core=core):
+                for k in (1, 2, 3):
+                    for p in range(3):
+                        copy = hand_on(k, p)[core]
+                        if copy is not None:
+                            copy.wait_send()
+                    v_hand_on[k][core].wait_send()
+
     roots[0] = root
     root_out = [
         remote(roots.at[0], roots.at[d], rsend.at[d], rrecv.at[d], at_behind(d)) for d in (7, 6, 5, 4, 3, 2, 1)
     ]
     start(root_out)
+    v_facing.wait_recv()
+    by_core(v_hand_on[1], go)
+    v_down.wait_recv()
+    by_core(v_hand_on[2], go)
+    v_on_down.wait_recv()
+    by_core(v_hand_on[3], go)
+    tiles_have_left()
     for d in (1, 3, 5, 7):
         vectors(0, d, 0, sibling).wait_recv()
     arrive(root_out)
@@ -482,13 +512,18 @@
     step_b(1)
     step_d(0)
     step_c(1)
+    left_all(root_out)
+    all_left(xs2, x2s, x2r, sent_2)
+    left_all(copies_b(0) + copies_c(0))
     step_e(0)
     step_d(1)
     gram_1 = collect(0)
     augmented = jnp.where(left, gram_1, jnp.where(lane == row + VEC, 1.0, 0.0))
     blocks = eliminate([augmented[8 * i : 8 * i + 8] for i in range(8)], 0, VEC)
     inverse_1 = jnp.where(left, 0.0, finish(blocks))
+    left_all(copies_d(0) + copies_e(0) + copies_b(1) + copies_c(1))
     step_e(1)
+    left_all(copies_d(1))
     gram_2 = jnp.where(left, 0.0, collect(1))
     half_way = dot32(inverse_1, jnp.concatenate([zeros, gram_2], axis=0))
     middle = dot32(half_way, jnp.concatenate([inverse_1, zeros], axis=0), NT)
@@ -496,43 +531,7 @@
     blocks = eliminate([augmented[8 * i : 8 * i + 8] for i in range(8)], 0, VEC)
     inverse_2 = jnp.where(left, 0.0, finish(blocks))
     out[...] = dot32(inverse_2, jnp.concatenate([jnp.zeros((VEC, TILE), F32), scaled_2], axis=0))
-
-    for copy in note_out:
-        copy.wait_send()
-    for j in range(6):
-        when(comes_down(j), left_here, own_down[j])
-        own_facing[j].wait_send()
-        if j < 3:
-            when(both(odd, up_to(j, THIRD)) if j in ACROSS else up_to(j, THIRD), left_here, on_down[j])
-        if j in ACROSS:
-            when(both(odd, up_to(j, THIRD)), left_here, across[j])
-
-    @pl.when(c == 0)
-    def _():
-        far_tile.wait_send()
-
-    @pl.when(c == 1)
-    def _():
-        for copy in near_tiles:
-            copy.wait_send()
-
-    for copy in [v_down] + root_out:
-        copy.wait_send()
-    v_facing.wait_send()
-    when(odd, left_here, v_across)
-    when(odd, left_here, v_on_down)
-    when(c == 0, left_here, v_far)
-    when(c == 1, left_here, v_near)
-    for k in (1, 2, 3):
-        by_core(v_hand_on[k], left_here)
-    all_left(xs2, x2s, x2r, sent_2)
-    for k in (1, 2, 3):
-        for p in range(3):
-            by_core(hand_on(k, p), left_here)
-    for i in range(2):
-        for copies in (copies_b, copies_c, copies_d, copies_e):
-            for copy in copies(i):
-                copy.wait_send()
+    left_all(copies_e(1))
 
 
 def shards(tile_values, tile_offset, tile_exponent, initial_vectors):

time: 81.1 us -> 79.6 us (0.982)
  Pallas kernels: 78.8 us -> 77.4 us
    pallas_call x1, Pallas kernels: 78.8 us -> 77.4 us  [shards(): pl.pallas_call(kernel, out_shape=jax.ShapeDtypeStruct((VEC, TILE), F32),...]
where the time goes in v5:
time: 79.6 us; the launch traced here: 79.5 us
  Pallas kernels  77.4 us (97%)
  local copies, waits for them, and re-layouts  2.06 us (3%)
    pallas_call x1, Pallas kernels, shards(): pl.pallas_call(kernel, out_shape=jax.ShapeDtypeStruct((VEC, TILE), F32),...  77.4 us
    unnamed x7, local copies, waits for them, and re-layouts  2.06 us

profile of v5, /device:TPU:1, one launch (start us, length us, event | category | flops | bytes accessed | tf_op | source)
XLA Modules:
  0.0 79.5 jit_solution(3602378427968744531)
XLA Ops:
  0.0 0.0 copy-start.2
  0.0 0.0 copy-start.1
  0.0 0.7 copy-done.2
  0.7 0.0 copy-done.1
  0.7 0.0 copy-start
  0.7 0.8 copy-done
  1.4 77.4 %embed.1 = f32[64,256]{1,0:T(8,128)S(1)} custom-call(bf16[1,6,256,256]{3,2,1,0:T(8,128)(2,1)} %tv.1, s32[1,6]{1,0:T(1,128)S(1)} %copy-done.1, s32[1,6]{1,0:T(1,128)S(1)} %copy-done.2, bf16[64,256]{1,0:T(8,128)(2,1)S(1)} %bitcast.3), custom_call_target="tpu_custom_call" | custom-call | flops 1200000000 | bytes 1000000 | tf_op jit(solution)/shard_map/embed/pallas_call | solution.py:540
  78.8 0.6 copy.6
Async XLA Ops:
  0.0 0.7 copy-start.2
  0.0 0.7 copy-start.1
  0.7 0.8 copy-start

commit v6 on v5

--- a/solution.py
+++ b/solution.py
@@ -151,6 +151,14 @@
             device_id=dev, device_id_type=pl.DeviceIdType.MESH,
         )
 
+    barrier = pltpu.get_barrier_semaphore()
+    met = y_mates + z_mates[:5] + x_mates[1:] + x_others[1:3]
+    for d in range(REACH - 1, 0, -1):
+        met.append(at_behind(d))
+        met.append(at_behind(-d))
+    for dev in met:
+        pl.semaphore_signal(barrier, inc=1, device_id=dev, device_id_type=pl.DeviceIdType.MESH)
+
     load_own = pltpu.make_async_copy(tv.at[0], own, own_sem)
     load_own.start()
     load_off = pltpu.make_async_copy(off_any, off, in_sem.at[0])
@@ -160,13 +168,6 @@
     load_v0 = pltpu.make_async_copy(v0, vs.at[0], in_sem.at[2])
     load_v0.start()
 
-    barrier = pltpu.get_barrier_semaphore()
-    met = y_mates + z_mates[:5] + x_mates[1:] + x_others[1:3]
-    for d in range(REACH - 1, 0, -1):
-        met.append(at_behind(d))
-        met.append(at_behind(-d))
-    for dev in met:
-        pl.semaphore_signal(barrier, inc=1, device_id=dev, device_id_type=pl.DeviceIdType.MESH)
     load_off.wait()
     load_ex.wait()
     offs = [off[0, s] for s in range(SLOTS)]
@@ -346,9 +347,9 @@
         far = remote(xs.at[0], xs.at[7], ssem.at[4], rsem.at[7], cross)
         near = remote(xs.at[0], xs.at[1], ssem.at[5], rsem.at[1], sibling)
         direct[2].start()
-        by_core([far, near], go)
         direct[1].start()
         direct[0].start()
+        by_core([far, near], go)
         return direct
 
     def passing(xs, ssem, rsem, k):

time: 79.6 us -> 79.3 us (level)
  no operation moved by 1% of the time
where the time goes in v6:
time: 79.3 us; the launch traced here: 79.1 us
  Pallas kernels  77.1 us (97%)
  local copies, waits for them, and re-layouts  2.06 us (3%)
    pallas_call x1, Pallas kernels, shards(): pl.pallas_call(kernel, out_shape=jax.ShapeDtypeStruct((VEC, TILE), F32),...  77.1 us
    unnamed x7, local copies, waits for them, and re-layouts  2.06 us

profile of v6, /device:TPU:1, one launch (start us, length us, event | category | flops | bytes accessed | tf_op | source)
XLA Modules:
  0.0 79.1 jit_solution(17415918484153663396)
XLA Ops:
  0.0 0.0 copy-start.2
  0.0 0.0 copy-start.1
  0.0 0.7 copy-done.2
  0.7 0.0 copy-done.1
  0.7 0.0 copy-start
  0.7 0.8 copy-done
  1.4 77.1 %embed.1 = f32[64,256]{1,0:T(8,128)S(1)} custom-call(bf16[1,6,256,256]{3,2,1,0:T(8,128)(2,1)} %tv.1, s32[1,6]{1,0:T(1,128)S(1)} %copy-done.1, s32[1,6]{1,0:T(1,128)S(1)} %copy-done.2, bf16[64,256]{1,0:T(8,128)(2,1)S(1)} %bitcast.3), custom_call_target="tpu_custom_call" | custom-call | flops 1200000000 | bytes 1000000 | tf_op jit(solution)/shard_map/embed/pallas_call | solution.py:541
  78.5 0.6 copy.6
Async XLA Ops:
  0.0 0.7 copy-start.2
  0.0 0.7 copy-start.1
  0.7 0.8 copy-start

commit v7 on v6

--- a/solution.py
+++ b/solution.py
@@ -326,7 +326,7 @@
         when(up_to(j, THIRD), has_come, on_down[j])
     by_core(hand_on(3, 0), go)
     absorb(6, rb6, False)
-    for d in (1, 3, 5, 7):
+    for d in (5, 7, 3, 1):
         here(d)
         absorb(d, rb[d], False)
 

time: 79.3 us -> 80.1 us (1.010)
  no operation moved by 1% of the time
where the time goes in v7:
time: 80.1 us; the launch traced here: 79.9 us
  Pallas kernels  77.9 us (97%)
  local copies, waits for them, and re-layouts  2.06 us (3%)
    pallas_call x1, Pallas kernels, shards(): pl.pallas_call(kernel, out_shape=jax.ShapeDtypeStruct((VEC, TILE), F32),...  77.9 us
    unnamed x7, local copies, waits for them, and re-layouts  2.06 us

profile of v7, /device:TPU:1, one launch (start us, length us, event | category | flops | bytes accessed | tf_op | source)
XLA Modules:
  0.0 79.9 jit_solution(9472990421184276256)
XLA Ops:
  0.0 0.0 copy-start.2
  0.0 0.0 copy-start.1
  0.0 0.7 copy-done.2
  0.7 0.0 copy-done.1
  0.7 0.0 copy-start
  0.7 0.8 copy-done
  1.4 77.9 %embed.1 = f32[64,256]{1,0:T(8,128)S(1)} custom-call(bf16[1,6,256,256]{3,2,1,0:T(8,128)(2,1)} %tv.1, s32[1,6]{1,0:T(1,128)S(1)} %copy-done.1, s32[1,6]{1,0:T(1,128)S(1)} %copy-done.2, bf16[64,256]{1,0:T(8,128)(2,1)S(1)} %bitcast.3), custom_call_target="tpu_custom_call" | custom-call | flops 1200000000 | bytes 1000000 | tf_op jit(solution)/shard_map/embed/pallas_call | solution.py:541
  79.3 0.6 copy.6
Async XLA Ops:
  0.0 0.7 copy-start.2
  0.0 0.7 copy-start.1
  0.7 0.8 copy-start
